TPU v7x, 32 devices: a whole 2x2x4 slice. The times are simulated.
32 devices in a mesh: member: 2 (over x), mesh: 8 (over z, y), writer: 2 (over core).
Axes of the slice: x: 2, y: 2, z: 4, core: 2. Of those that a mesh axis runs over, the one named last changes fastest.
Arguments:
- mesh_nodes: bfloat16 [16384, 512], P(('member', 'mesh'), 'writer'), parts along dimension 0, may hold values from -6 to 6
- grid_state: bfloat16 [80, 131072], P(None, ('member', 'mesh', 'writer')), parts along dimension 1, may hold values from -6 to 6
- interp: bfloat16 [512, 4, 128, 128], P('mesh'), may hold values from -0.25 to 0.25
- wanted: int32 [8, 32], P('mesh'), may hold values from 0 to 63, as said below
- tile_slots: int32 [512, 4], P('mesh'), may hold values from 0 to 31
- edge_count: int32 [512], P('mesh'), may hold values from 1 to 4
- w_in: bfloat16 [512, 512], replicated, may hold values from -0.25 to 0.25
- b_in: bfloat16 [512], replicated, may hold values from -4 to 4
- w_out: bfloat16 [512, 80], replicated, may hold values from -0.25 to 0.25
- b_out: bfloat16 [80], replicated, may hold values from -2 to 2
- writer_order: int32 [80], replicated, may hold values from 0 to 79, each once
Outputs:
- written: bfloat16 [80, 131072], P('writer', ('member', 'mesh')), parts along dimension 1
There are 2 independent parts, one for each index of `member`. A program takes and returns all parts, laid end to end along the dimension named above; an argument that names none is the same for every part. Nothing has to cross between parts.
Inputs may be any that keep to these rules, and one draw needn't show every extreme that they name: `wanted`: each row lists 32 different node blocks; at most 8 of them lie among the 8 blocks of one index of mesh, and exactly 8 do for one index, in every row.
All inputs are finite; a program needn't handle non-finite values.
Results may differ from a plain program's by a relative error of at most 0.0039.
Values may be sent and summed in bfloat16 or wider, within the bound.
No kernel may reach another device: no remote copies, remote signals or barrier semaphores. Data moves between devices by JAX's collectives and lax.ppermute only.
A program may use at most 128 MiB of HBM per device.

v0:
```python
import jax
import jax.numpy as jnp
from jax import lax
from jax.experimental import pallas as pl
from jax.experimental.pallas import tpu as pltpu
from jax.sharding import PartitionSpec as P

BLK = 128
K = 4
GROUP = 4
META = 8


def ring_order(count, columns):
    if columns == 1:
        return list(range(count))
    return list(range(0, count, 2)) + list(range(count - 1, 0, -2))


def prepare_kernel(count, columns, blocks, wanted, slots, live, order, w_out, b_out, state, w_in, nodes, interp, *rest):
    meta, heads, bias, ordered, w_in_kept, nodes_kept, interp_kept, codes, sem = rest
    core = lax.axis_index("writer")
    tiles = live.shape[0] // 2
    first_tile = core * tiles
    pairs = [(w_in, w_in_kept), (nodes, nodes_kept)]
    eighth = max(tiles // 8, 1)
    for start in range(0, tiles, eighth):
        pairs.append((interp.at[pl.ds(first_tile + start, eighth)], interp_kept.at[pl.ds(start, eighth)]))
    kept = [pltpu.make_async_copy(source, target, sem.at[i]) for i, (source, target) in enumerate(pairs)]
    for copy in kept:
        copy.start()

    def place(index):
        if columns == 1:
            return index
        row = lax.shift_right_logical(index, 1)
        return jnp.where(lax.rem(index, 2) == 0, row, count - 1 - row)

    here = place(lax.axis_index("mesh"))
    first_stage = stages_of(count)[0]

    def locate(entry, _):
        block = wanted[0, entry]
        behind = here - place(lax.div(block, blocks))
        behind = jnp.where(core == 0, behind, -behind)
        behind = jnp.where(behind < 0, behind + count, behind)
        codes[entry] = behind * blocks + lax.rem(block, blocks)
        return 0

    lax.fori_loop(0, wanted.shape[1], locate, 0)
    stages = len(stages_of(count))
    for stage in range(stages):
        meta[tiles * META + stage * (tiles + 1)] = 0

    def describe(tile, _):
        number = first_tile + tile
        alive = live[number]
        stage = jnp.int32(first_stage)
        for k in range(K):
            code = codes[slots[k, number]]
            behind = lax.div(code, blocks)
            distance = jnp.minimum(behind, count - behind)
            stage = jnp.where(k < alive, jnp.maximum(stage, distance), stage)
            meta[tile * META + k] = code
        meta[tile * META + K] = alive
        meta[tile * META + K + 1] = number
        work = tiles * META + (stage - first_stage) * (tiles + 1)
        meta[work] = meta[work] + 1
        meta[work + meta[work]] = tile
        return 0

    lax.fori_loop(0, tiles, describe, 0)

    channels = state.shape[0]
    each = channels // 2
    rows = ordered.shape[0] // 2
    variable = lax.broadcasted_iota(jnp.int32, (channels, channels), 0)
    picks = jnp.where(variable == order[...], jnp.float32(1), jnp.float32(0)).T
    top, bottom = picks[:each], picks[each:]
    pad = jnp.zeros((rows - each, channels), jnp.float32)
    own, other = jnp.where(core == 0, top, bottom), jnp.where(core == 0, bottom, top)
    picks = jnp.concatenate([own, pad, other, pad], axis=0)
    bias[...] = jnp.sum(picks * b_out[...].astype(jnp.float32), axis=1, keepdims=True)
    picks = picks.astype(jnp.bfloat16)
    heads[...] = lax.dot_general(
        picks, w_out[...], (((1,), (0,)), ((), ())), preferred_element_type=jnp.float32
    ).astype(jnp.bfloat16)
    step = min(512, state.shape[1])
    for start in range(0, state.shape[1], step):
        part = jnp.dot(picks, state[:, start : start + step], preferred_element_type=jnp.float32)
        ordered[:, start : start + step] = part.astype(jnp.bfloat16)
    for copy in kept:
        copy.wait()


def in_hbm(array):
    return pltpu.with_memory_space_constraint(array, pltpu.HBM)


def prepare(count, columns, blocks, wanted, slots, live, order, w_out, b_out, state, w_in, nodes, interp):
    vmem, smem = pl.BlockSpec(memory_space=pltpu.VMEM), pl.BlockSpec(memory_space=pltpu.SMEM)
    rows = 2 * (-(-(state.shape[0] // 2) // 16) * 16)
    tiles = live.shape[0] // 2
    return pl.pallas_call(
        lambda *refs: prepare_kernel(count, columns, blocks, *refs),
        out_shape=[
            jax.ShapeDtypeStruct((tiles * META + len(stages_of(count)) * (tiles + 1),), jnp.int32),
            jax.ShapeDtypeStruct((rows, w_out.shape[1]), jnp.bfloat16),
            jax.ShapeDtypeStruct((rows, 1), jnp.float32),
            jax.ShapeDtypeStruct((rows, state.shape[1]), jnp.bfloat16),
            jax.ShapeDtypeStruct(w_in.shape, w_in.dtype),
            jax.ShapeDtypeStruct(nodes.shape, nodes.dtype),
            jax.ShapeDtypeStruct((tiles, *interp.shape[1:]), interp.dtype),
        ],
        in_specs=[smem] * 3 + [vmem] * 4 + [pl.BlockSpec(memory_space=pltpu.HBM)] * 3,
        out_specs=[smem] + [vmem] * 6,
        scratch_shapes=[pltpu.SMEM((wanted.shape[1],), jnp.int32), pltpu.SemaphoreType.DMA((2 + min(tiles, 8),))],
        compiler_params=pltpu.CompilerParams(vmem_limit_bytes=12 * 2**20),
        cost_estimate=pl.CostEstimate(flops=2 * rows * state.size, bytes_accessed=6 * state.size, transcendentals=0),
        name="prepare",
    )(*[in_hbm(x) for x in (wanted, slots, live, order, w_out, b_out, state, w_in, nodes, interp)])


def stages_of(count):
    far = count // 2
    return list(range(max(far - 2, 1), far + 1))


def decode_kernel(stage, blocks, pieces, tiles, held, *refs):
    meta, w_in, b_in, w_out, b_out, state, interp = refs[:7]
    piece_refs = refs[7 : 7 + 2 * len(pieces)]
    own_out, other_out, x_buf = refs[7 + held + 2 * len(pieces) :]
    half = piece_refs[0].shape[1]
    rows = own_out.shape[0]
    core = lax.axis_index("writer")

    def columns_of(tile):
        return pl.ds(pl.multiple_of(tile * BLK, BLK), BLK)

    def take_block(code, j, k, low, high):
        if high - low > 1:
            middle = (low + high) // 2
            below = code < pieces[middle] * blocks
            pl.when(below)(lambda: take_block(code, j, k, low, middle))
            pl.when(jnp.logical_not(below))(lambda: take_block(code, j, k, middle, high))
            return
        source = pl.ds(pl.multiple_of((code - pieces[low] * blocks) * BLK, BLK), BLK)
        for h in range(2):
            x_buf[j, k * BLK : (k + 1) * BLK, h * half : (h + 1) * half] = piece_refs[2 * low + h][source, :]

    work = tiles * META + stage * (tiles + 1)
    count = meta[work]

    def tile_at(i):
        return meta[work + 1 + i]

    def arrive(i, j):
        tile = tile_at(i)
        live = meta[tile * META + K]
        for k in range(K):

            @pl.when(k < live)
            def _():
                take_block(meta[tile * META + k], j, k, 0, len(pieces))

            @pl.when(k >= live)
            def _():
                x_buf[j, k * BLK : (k + 1) * BLK, :] = jnp.zeros((BLK, 2 * half), jnp.bfloat16)

    def group(g, _):
        for j in range(GROUP):

            @pl.when(GROUP * g + j < count)
            def _():
                arrive(GROUP * g + j, j)

        aggregated = []
        for j in range(GROUP):
            tile = tile_at(jnp.minimum(GROUP * g + j, count - 1))
            spread = jnp.concatenate([interp[tile, k] for k in range(K)], axis=1)
            aggregated.append(jnp.dot(spread, x_buf[j], preferred_element_type=jnp.float32).astype(jnp.bfloat16))
        aggregated = jnp.concatenate(aggregated, axis=0)
        layer = b_in[...].astype(jnp.float32)
        for h in range(2):
            features = pl.ds(pl.multiple_of((core if h == 0 else 1 - core) * half, half), half)
            layer = layer + jnp.dot(
                aggregated[:, h * half : (h + 1) * half], w_in[features, :], preferred_element_type=jnp.float32
            )
        hidden = (layer * (0.5 * jnp.tanh(0.5 * layer) + 0.5)).astype(jnp.bfloat16)
        decoded = lax.dot_general(
            w_out[...], hidden, (((1,), (1,)), ((), ())), preferred_element_type=jnp.float32
        )
        decoded = decoded + b_out[...]
        for j in range(GROUP):
            i = GROUP * g + j

            @pl.when(i < count)
            def _():
                tile = tile_at(i)
                before = state[:, columns_of(tile)].astype(jnp.float32)
                after = (before + decoded[:, j * BLK : (j + 1) * BLK]).astype(jnp.bfloat16)
                own_out[:, columns_of(tile)] = after[:rows]
                other_out[:, columns_of(tile)] = after[rows:]

        return 0

    lax.fori_loop(0, (count + GROUP - 1) // GROUP, group, 0)


def decode_tiles(stage, blocks, pieces, tiles, small, arrays, outs):
    flat = [half for pair in arrays for half in pair]
    half = flat[0].shape[1]
    state = small[-2]
    rows = state.shape[0] // 2
    vmem = pl.BlockSpec(memory_space=pltpu.VMEM)
    first_out = 7 + len(flat)
    share = max(tiles // 4, 1)
    return pl.pallas_call(
        lambda *refs: decode_kernel(stage, blocks, pieces, tiles, len(outs), *refs),
        out_shape=[jax.ShapeDtypeStruct((rows, state.shape[1]), jnp.bfloat16)] * 2,
        in_specs=[pl.BlockSpec(memory_space=pltpu.SMEM)] + [vmem] * (6 + len(flat) + len(outs)),
        out_specs=[vmem] * 2,
        input_output_aliases={first_out + j: j for j in range(len(outs))},
        scratch_shapes=[pltpu.VMEM((GROUP, K * BLK, 2 * half), jnp.bfloat16)],
        compiler_params=pltpu.CompilerParams(vmem_limit_bytes=16 * 2**20),
        cost_estimate=pl.CostEstimate(
            flops=share * BLK * 2 * (K * BLK * 2 * half + 4 * half * half + 4 * half * rows),
            bytes_accessed=share * 6 * BLK * BLK * 10,
            transcendentals=share * BLK * 2 * half,
        ),
        name="decode_tiles",
    )(*small, *flat, *outs)


def make_local(count):
    columns = 2 if count == 8 else 1
    far = count // 2
    ring = ring_order(count, columns)
    onward = []
    for place in range(count):
        onward.append((ring[place] * 2, ring[(place + 1) % count] * 2))
        onward.append((ring[place] * 2 + 1, ring[(place - 1) % count] * 2 + 1))

    def send_on(piece):
        return lax.ppermute(piece, ("mesh", "writer"), onward)

    def swap(piece):
        return lax.ppermute(piece, "writer", [(0, 1), (1, 0)])

    def local(
        mesh_nodes,
        grid_state,
        interp,
        wanted,
        tile_slots,
        edge_count,
        w_in,
        b_in,
        w_out,
        b_out,
        writer_order,
    ):
        nodes = mesh_nodes.shape[0]
        blocks = nodes // BLK
        core = lax.axis_index("writer")
        tiles = interp.shape[0] // 2
        each = w_out.shape[1] // 2
        stages = stages_of(count)
        meta, heads, bias, state, w_in, nodes_kept, interp_kept = prepare(
            count,
            columns,
            blocks,
            wanted,
            tile_slots.T,
            edge_count,
            writer_order[None],
            w_out.T,
            b_out[None],
            grid_state,
            w_in,
            mesh_nodes,
            interp,
        )
        small = (meta, w_in, b_in[None], heads, bias, state, interp_kept)
        outs = []

        other_nodes = swap(mesh_nodes)
        same, cross = [mesh_nodes], [other_nodes]
        table = {0: (nodes_kept, other_nodes)}
        def decode(d, outs):
            pieces = [p for p in sorted(table) if min(p, count - p) <= d]
            return list(
                decode_tiles(stages.index(d), blocks, pieces, tiles, small, [table[p] for p in pieces], outs)
            )

        for d in range(1, far + 1):
            if d == 2:
                same[-1], small = lax.optimization_barrier((same[-1], small))
            same.append(send_on(same[-1]))
            if d < far:
                cross.append(send_on(cross[-1]))
            swapped = (cross[-1], same[-1])
            if d - 1 in stages:
                outs = decode(d - 1, outs)
                if d < far:
                    *swapped, outs = lax.optimization_barrier((*swapped, outs))
            if d < far:
                table[d] = (same[d], cross[d])
                table[count - d] = (swap(swapped[0]), swap(swapped[1]))
            else:
                table[d] = (same[d], swap(swapped[1]))
        outs = decode(far, outs)
        received = swap(outs[1])
        own, received = outs[0][:each], received[:each]
        return jnp.concatenate(
            [jnp.where(core == 0, own, received), jnp.where(core == 0, received, own)], axis=1
        )

    return local


def solution(mesh):
    placed = (
        P(("member", "mesh"), "writer"),
        P(None, ("member", "mesh", "writer")),
        P("mesh", None, None, None),
        P("mesh", None),
        P("mesh", None),
        P("mesh"),
        P(),
        P(),
        P(),
        P(),
        P(),
    )
    return jax.shard_map(
        make_local(mesh.shape["mesh"]),
        mesh=mesh,
        in_specs=placed,
        out_specs=P("writer", ("member", "mesh")),
        check_vma=False,
    )
```

profile of v0, /device:TPU:29, one launch (start us, length us, event | category | flops | bytes accessed | tf_op | source)
XLA Modules:
  0.0 60.4 jit_solution(18326009619962925982)
XLA Ops:
  0.0 0.7 %collective-permute-start.1 = (bf16[1024,256]{1,0:T(8,128)(2,1)}, bf16[1024,256]{1,0:T(8,128)(2,1)S(1)}, u32[]{:S(2)}, u32[]{:S(2)}) collective-permute-start(bf16[1024,256]{1,0:T(8,128)(2,1)} %refs_8_.1), channel_id=1, source_target_pairs={{0,1},{1,0},{2,3},{3,2},{4,5},{5,4},{6,7},{7,6},{8,9},{9,8},{10,11... | collective-permute-start | bytes 1572872 | tf_op jit(solution)/shard_map/ppermute | solution.py:248
  0.7 0.2 collective-permute-start
  0.9 1.5 %collective-permute-done.1.refs_8_ = bf16[1024,256]{1,0:T(8,128)(2,1)S(1)} collective-permute-done((bf16[1024,256]{1,0:T(8,128)(2,1)}, bf16[1024,256]{1,0:T(8,128)(2,1)S(1)}, u32[]{:S(2)}, u32[]{:S(2)}) %collective-permute-start.1) | collective-permute-done | bytes 524320 | tf_op jit(solution)/shard_map/ppermute | solution.py:248
  2.4 0.2 collective-permute-start.2
  2.7 0.7 %broadcast_in_dim.11.refs_2_ = bf16[1,512]{1,0:T(2,128)(2,1)S(1)} reshape(bf16[512]{0:T(512)(128)(2,1)} %param.18) | data formatting | bytes 2048 | tf_op jit(solution)/shard_map/broadcast_in_dim | solution.py:284
  3.3 4.3 %prepare.1 = (s32[355]{0:T(512)S(1)}, bf16[96,512]{1,0:T(8,128)(2,1)S(1)}, f32[96,1]{1,0:T(8,128)S(1)}, bf16[96,4096]{1,0:T(8,128)(2,1)S(1)}, bf16[512,512]{1,0:...) custom-call(s32[1,32]{1,0:T(1,128)} %refs_0_.1, s32[4,64]{1,0:T(4,128)} %bitcast.5, ...), custom_call_target="tpu_custom_call" | custom-call | flops 62914560 | bytes 1966080 | tf_op jit(solution)/shard_map/prepare/pallas_call | solution.py:104
  7.7 1.5 %collective-permute-done.refs_9_ = bf16[1024,256]{1,0:T(8,128)(2,1)S(1)} collective-permute-done((bf16[1024,256]{1,0:T(8,128)(2,1)}, bf16[1024,256]{1,0:T(8,128)(2,1)S(1)}, u32[]{:S(2)}, u32[]{:S(2)}) %collective-permute-start) | collective-permute-done | bytes 524320 | tf_op jit(solution)/shard_map/ppermute | solution.py:245
  9.2 0.2 collective-permute-start.3
  9.4 5.4 %collective-permute-done.2.refs_10_ = bf16[1024,256]{1,0:T(8,128)(2,1)S(1)} collective-permute-done((bf16[1024,256]{1,0:T(8,128)(2,1)S(1)}, bf16[1024,256]{1,0:T(8,128)(2,1)S(1)}, u32[]{:S(2)}, u32[]{:S(2)}) %collective-permute-start.2) | collective-permute-done | bytes 524320 | tf_op jit(solution)/shard_map/ppermute | solution.py:245
  14.8 0.2 collective-permute-start.4
  15.1 1.1 %collective-permute-start.12 = (bf16[1024,256]{1,0:T(8,128)(2,1)S(1)}, bf16[1024,256]{1,0:T(8,128)(2,1)S(1)}, u32[]{:S(2)}, u32[]{:S(2)}) collective-permute-start(bf16[1024,256]{1,0:T(8,128)(2,1)S(1)} %collective-permute-done.refs_9_), channel_id=1, source_target_pairs={{0,1},{1,0},{2,3},{3,2},{4,5},{5,4},{6,7},{7,6},{8,9},{9,8},{10,11... | collective-permute-start | bytes 1572872 | tf_op jit(solution)/shard_map/ppermute | solution.py:248
  16.1 4.3 %collective-permute-done.3.refs_11_ = bf16[1024,256]{1,0:T(8,128)(2,1)S(1)} collective-permute-done((bf16[1024,256]{1,0:T(8,128)(2,1)S(1)}, bf16[1024,256]{1,0:T(8,128)(2,1)S(1)}, u32[]{:S(2)}, u32[]{:S(2)}) %collective-permute-start.3) | collective-permute-done | bytes 524320 | tf_op jit(solution)/shard_map/ppermute | solution.py:245
  20.4 0.2 collective-permute-start.5
  20.7 1.1 %collective-permute-start.10 = (bf16[1024,256]{1,0:T(8,128)(2,1)S(1)}, bf16[1024,256]{1,0:T(8,128)(2,1)S(1)}, u32[]{:S(2)}, u32[]{:S(2)}) collective-permute-start(bf16[1024,256]{1,0:T(8,128)(2,1)S(1)} %collective-permute-done.3.refs_11_), channel_id=1, source_target_pairs={{0,1},{1,0},{2,3},{3,2},{4,5},{5,4},{6,7},{7,6},{8,9},{9,8},{10,11... | collective-permute-start | bytes 1572872 | tf_op jit(solution)/shard_map/ppermute | solution.py:248
  21.8 0.0 collective-permute-start.11
  21.8 4.3 %collective-permute-done.4.refs_12_ = bf16[1024,256]{1,0:T(8,128)(2,1)S(1)} collective-permute-done((bf16[1024,256]{1,0:T(8,128)(2,1)S(1)}, bf16[1024,256]{1,0:T(8,128)(2,1)S(1)}, u32[]{:S(2)}, u32[]{:S(2)}) %collective-permute-start.4) | collective-permute-done | bytes 524320 | tf_op jit(solution)/shard_map/ppermute | solution.py:245
  26.1 0.9 %collective-permute-start.9 = (bf16[1024,256]{1,0:T(8,128)(2,1)S(1)}, bf16[1024,256]{1,0:T(8,128)(2,1)S(1)}, u32[]{:S(2)}, u32[]{:S(2)}) collective-permute-start(bf16[1024,256]{1,0:T(8,128)(2,1)S(1)} %collective-permute-done.4.refs_12_), channel_id=1, source_target_pairs={{0,1},{1,0},{2,3},{3,2},{4,5},{5,4},{6,7},{7,6},{8,9},{9,8},{10,11... | collective-permute-start | bytes 1572872 | tf_op jit(solution)/shard_map/ppermute | solution.py:248
  26.9 0.0 collective-permute-done.12.refs_16_.refs_20_.refs_22_
  26.9 0.2 collective-permute-start.6
  27.2 4.5 %collective-permute-done.5.refs_13_ = bf16[1024,256]{1,0:T(8,128)(2,1)S(1)} collective-permute-done((bf16[1024,256]{1,0:T(8,128)(2,1)S(1)}, bf16[1024,256]{1,0:T(8,128)(2,1)S(1)}, u32[]{:S(2)}, u32[]{:S(2)}) %collective-permute-start.5) | collective-permute-done | bytes 524320 | tf_op jit(solution)/shard_map/ppermute | solution.py:245
  31.7 0.2 collective-permute-start.7
  31.9 0.0 collective-permute-done.10.refs_14_.refs_18_.refs_20_
  31.9 0.0 collective-permute-done.11.refs_15_.refs_19_.refs_21_
  31.9 0.0 collective-permute-done.9.refs_13_.refs_17_.refs_19_
  31.9 1.9 %decode_tiles.3 = (bf16[48,4096]{1,0:T(8,128)(2,1)S(1)}, bf16[48,4096]{1,0:T(8,128)(2,1)S(1)}) custom-call(s32[355]{0:T(512)S(1)} %get-tuple-element.36.refs_0_, bf16[512,512]{1,0:T(8,128)(2,1)S(1)} %get-tuple-element.37.refs_1_, bf16[1,512]{1,0:T(2,128)(2,1)S(1)} %broadcast_in_dim.11.refs_2_, bf16[96,512]{1,0:T(8,128)(2,1)S(1)} %get-tuple-element.39.refs_3_, ...), custom_call_target="tpu_custom_call" | custom-call | flops 1174405120 | bytes 7864320 | tf_op jit(solution)/shard_map/decode_tiles/pallas_call | solution.py:218
  33.9 3.4 %collective-permute-done.6.refs_14_ = bf16[1024,256]{1,0:T(8,128)(2,1)S(1)} collective-permute-done((bf16[1024,256]{1,0:T(8,128)(2,1)S(1)}, bf16[1024,256]{1,0:T(8,128)(2,1)S(1)}, u32[]{:S(2)}, u32[]{:S(2)}) %collective-permute-start.6) | collective-permute-done | bytes 524320 | tf_op jit(solution)/shard_map/ppermute | solution.py:245
  37.3 0.9 %collective-permute-start.13 = (bf16[1024,256]{1,0:T(8,128)(2,1)S(1)}, bf16[1024,256]{1,0:T(8,128)(2,1)S(1)}, u32[]{:S(2)}, u32[]{:S(2)}) collective-permute-start(bf16[1024,256]{1,0:T(8,128)(2,1)S(1)} %collective-permute-done.6.refs_14_), channel_id=1, source_target_pairs={{0,1},{1,0},{2,3},{3,2},{4,5},{5,4},{6,7},{7,6},{8,9},{9,8},{10,11... | collective-permute-start | bytes 1572872 | tf_op jit(solution)/shard_map/ppermute | solution.py:248
  38.2 0.0 collective-permute-start.14
  38.2 4.8 %collective-permute-done.7.refs_15_ = bf16[1024,256]{1,0:T(8,128)(2,1)S(1)} collective-permute-done((bf16[1024,256]{1,0:T(8,128)(2,1)S(1)}, bf16[1024,256]{1,0:T(8,128)(2,1)S(1)}, u32[]{:S(2)}, u32[]{:S(2)}) %collective-permute-start.7) | collective-permute-done | bytes 524320 | tf_op jit(solution)/shard_map/ppermute | solution.py:245
  42.9 0.9 %collective-permute-start.8 = (bf16[1024,256]{1,0:T(8,128)(2,1)S(1)}, bf16[1024,256]{1,0:T(8,128)(2,1)S(1)}, u32[]{:S(2)}, u32[]{:S(2)}) collective-permute-start(bf16[1024,256]{1,0:T(8,128)(2,1)S(1)} %collective-permute-done.7.refs_15_), channel_id=1, source_target_pairs={{0,1},{1,0},{2,3},{3,2},{4,5},{5,4},{6,7},{7,6},{8,9},{9,8},{10,11... | collective-permute-start | bytes 1572872 | tf_op jit(solution)/shard_map/ppermute | solution.py:248
  43.8 0.0 collective-permute-done.13.refs_15_.refs_17_
  43.8 0.0 collective-permute-done.14.refs_16_.refs_18_
  43.8 10.1 %decode_tiles.4 = (bf16[48,4096]{1,0:T(8,128)(2,1)S(1)}, bf16[48,4096]{1,0:T(8,128)(2,1)S(1)}) custom-call(s32[355]{0:T(512)S(1)} %get-tuple-element.36.refs_0_, bf16[512,512]{1,0:T(8,128)(2,1)S(1)} %get-tuple-element.37.refs_1_, bf16[1,512]{1,0:T(2,128)(2,1)S(1)} %broadcast_in_dim.11.refs_2_, ...), custom_call_target="tpu_custom_call", output_to_operand_aliasing={{0}: (21, {}), {1}: (22, {})} | custom-call | flops 1174405120 | bytes 7864320 | tf_op jit(solution)/shard_map/decode_tiles/pallas_call | solution.py:218
  53.9 0.0 collective-permute-done.8.refs_16_
  53.9 3.8 %decode_tiles.5 = (bf16[48,4096]{1,0:T(8,128)(2,1)S(1)}, bf16[48,4096]{1,0:T(8,128)(2,1)S(1)}) custom-call(s32[355]{0:T(512)S(1)} %get-tuple-element.36.refs_0_, bf16[512,512]{1,0:T(8,128)(2,1)S(1)} %get-tuple-element.37.refs_1_, bf16[1,512]{1,0:T(2,128)(2,1)S(1)} %broadcast_in_dim.11.refs_2_, ...), custom_call_target="tpu_custom_call", output_to_operand_aliasing={{0}: (23, {}), {1}: (24, {})} | custom-call | flops 1174405120 | bytes 7864320 | tf_op jit(solution)/shard_map/decode_tiles/pallas_call | solution.py:218
  57.7 0.1 collective-permute-start.15
  57.8 1.7 %collective-permute-done.15 = bf16[48,4096]{1,0:T(8,128)(2,1)S(1)} collective-permute-done((bf16[48,4096]{1,0:T(8,128)(2,1)S(1)}, bf16[48,4096]{1,0:T(8,128)(2,1)S(1)}, u32[]{:S(2)}, u32[]{:S(2)}) %collective-permute-start.15) | collective-permute-done | bytes 393248 | tf_op jit(solution)/shard_map/ppermute | solution.py:248
  59.5 0.9 %pad_maximum_fusion = bf16[40,8192]{1,0:T(8,128)(2,1)} fusion(bf16[40,4096]{1,0:T(8,128)(2,1)S(1)} %get-tuple-element.56, bf16[40,4096]{1,0:T(8,128)(2,1)S(1)} %get-tuple-element.55), kind=kLoop, calls=%fused_computation | loop fusion | flops 1310720 | bytes 1310720 | tf_op jit(solution)/shard_map/concatenate | solution.py:315
  (1 shorter events, 0.0 us)
Async XLA Ops:
  0.0 2.4 %collective-permute-start.1 = (bf16[1024,256]{1,0:T(8,128)(2,1)}, bf16[1024,256]{1,0:T(8,128)(2,1)S(1)}, u32[]{:S(2)}, u32[]{:S(2)}) collective-permute-start(bf16[1024,256]{1,0:T(8,128)(2,1)} %refs_8_.1), channel_id=1, source_target_pairs={{0,1},{1,0},{2,3},{3,2},{4,5},{5,4},{6,7},{7,6},{8,9},{9,8},{10,11... | collective-permute-start | bytes 1572872 | tf_op jit(solution)/shard_map/ppermute | solution.py:248
  0.7 8.5 %collective-permute-start = (bf16[1024,256]{1,0:T(8,128)(2,1)}, bf16[1024,256]{1,0:T(8,128)(2,1)S(1)}, u32[]{:S(2)}, u32[]{:S(2)}) collective-permute-start(bf16[1024,256]{1,0:T(8,128)(2,1)} %refs_8_.1), channel_id=1, source_target_pairs={{0,4},{1,3},{4,8},{5,1},{8,12},{9,5},{12,14},{13,9},{14,10},{15,13... | collective-permute-start | bytes 1572872 | tf_op jit(solution)/shard_map/ppermute | solution.py:245
  2.4 12.4 %collective-permute-start.2 = (bf16[1024,256]{1,0:T(8,128)(2,1)S(1)}, bf16[1024,256]{1,0:T(8,128)(2,1)S(1)}, u32[]{:S(2)}, u32[]{:S(2)}) collective-permute-start(bf16[1024,256]{1,0:T(8,128)(2,1)S(1)} %collective-permute-done.1.refs_8_), channel_id=1, source_target_pairs={{0,4},{1,3},{4,8},{5,1},{8,12},{9,5},{12,14},{13,9},{14,10},{15,13... | collective-permute-start | bytes 1572872 | tf_op jit(solution)/shard_map/ppermute | solution.py:245
  9.2 11.2 %collective-permute-start.3 = (bf16[1024,256]{1,0:T(8,128)(2,1)S(1)}, bf16[1024,256]{1,0:T(8,128)(2,1)S(1)}, u32[]{:S(2)}, u32[]{:S(2)}) collective-permute-start(bf16[1024,256]{1,0:T(8,128)(2,1)S(1)} %collective-permute-done.refs_9_), channel_id=1, source_target_pairs={{0,4},{1,3},{4,8},{5,1},{8,12},{9,5},{12,14},{13,9},{14,10},{15,13... | collective-permute-start | bytes 1572872 | tf_op jit(solution)/shard_map/ppermute | solution.py:245
  14.8 11.2 %collective-permute-start.4 = (bf16[1024,256]{1,0:T(8,128)(2,1)S(1)}, bf16[1024,256]{1,0:T(8,128)(2,1)S(1)}, u32[]{:S(2)}, u32[]{:S(2)}) collective-permute-start(bf16[1024,256]{1,0:T(8,128)(2,1)S(1)} %collective-permute-done.2.refs_10_), channel_id=1, source_target_pairs={{0,4},{1,3},{4,8},{5,1},{8,12},{9,5},{12,14},{13,9},{14,10},{15,13... | collective-permute-start | bytes 1572872 | tf_op jit(solution)/shard_map/ppermute | solution.py:245
  15.1 11.9 %collective-permute-start.12 = (bf16[1024,256]{1,0:T(8,128)(2,1)S(1)}, bf16[1024,256]{1,0:T(8,128)(2,1)S(1)}, u32[]{:S(2)}, u32[]{:S(2)}) collective-permute-start(bf16[1024,256]{1,0:T(8,128)(2,1)S(1)} %collective-permute-done.refs_9_), channel_id=1, source_target_pairs={{0,1},{1,0},{2,3},{3,2},{4,5},{5,4},{6,7},{7,6},{8,9},{9,8},{10,11... | collective-permute-start | bytes 1572872 | tf_op jit(solution)/shard_map/ppermute | solution.py:248
  20.4 11.2 %collective-permute-start.5 = (bf16[1024,256]{1,0:T(8,128)(2,1)S(1)}, bf16[1024,256]{1,0:T(8,128)(2,1)S(1)}, u32[]{:S(2)}, u32[]{:S(2)}) collective-permute-start(bf16[1024,256]{1,0:T(8,128)(2,1)S(1)} %collective-permute-done.3.refs_11_), channel_id=1, source_target_pairs={{0,4},{1,3},{4,8},{5,1},{8,12},{9,5},{12,14},{13,9},{14,10},{15,13... | collective-permute-start | bytes 1572872 | tf_op jit(solution)/shard_map/ppermute | solution.py:245
  20.7 11.2 %collective-permute-start.10 = (bf16[1024,256]{1,0:T(8,128)(2,1)S(1)}, bf16[1024,256]{1,0:T(8,128)(2,1)S(1)}, u32[]{:S(2)}, u32[]{:S(2)}) collective-permute-start(bf16[1024,256]{1,0:T(8,128)(2,1)S(1)} %collective-permute-done.3.refs_11_), channel_id=1, source_target_pairs={{0,1},{1,0},{2,3},{3,2},{4,5},{5,4},{6,7},{7,6},{8,9},{9,8},{10,11... | collective-permute-start | bytes 1572872 | tf_op jit(solution)/shard_map/ppermute | solution.py:248
  21.8 10.2 %collective-permute-start.11 = (bf16[1024,256]{1,0:T(8,128)(2,1)S(1)}, bf16[1024,256]{1,0:T(8,128)(2,1)S(1)}, u32[]{:S(2)}, u32[]{:S(2)}) collective-permute-start(bf16[1024,256]{1,0:T(8,128)(2,1)S(1)} %collective-permute-done.2.refs_10_), channel_id=1, source_target_pairs={{0,1},{1,0},{2,3},{3,2},{4,5},{5,4},{6,7},{7,6},{8,9},{9,8},{10,11... | collective-permute-start | bytes 1572872 | tf_op jit(solution)/shard_map/ppermute | solution.py:248
  26.1 5.9 %collective-permute-start.9 = (bf16[1024,256]{1,0:T(8,128)(2,1)S(1)}, bf16[1024,256]{1,0:T(8,128)(2,1)S(1)}, u32[]{:S(2)}, u32[]{:S(2)}) collective-permute-start(bf16[1024,256]{1,0:T(8,128)(2,1)S(1)} %collective-permute-done.4.refs_12_), channel_id=1, source_target_pairs={{0,1},{1,0},{2,3},{3,2},{4,5},{5,4},{6,7},{7,6},{8,9},{9,8},{10,11... | collective-permute-start | bytes 1572872 | tf_op jit(solution)/shard_map/ppermute | solution.py:248
  26.9 10.4 %collective-permute-start.6 = (bf16[1024,256]{1,0:T(8,128)(2,1)S(1)}, bf16[1024,256]{1,0:T(8,128)(2,1)S(1)}, u32[]{:S(2)}, u32[]{:S(2)}) collective-permute-start(bf16[1024,256]{1,0:T(8,128)(2,1)S(1)} %collective-permute-done.4.refs_12_), channel_id=1, source_target_pairs={{0,4},{1,3},{4,8},{5,1},{8,12},{9,5},{12,14},{13,9},{14,10},{15,13... | collective-permute-start | bytes 1572872 | tf_op jit(solution)/shard_map/ppermute | solution.py:245
  31.7 11.2 %collective-permute-start.7 = (bf16[1024,256]{1,0:T(8,128)(2,1)S(1)}, bf16[1024,256]{1,0:T(8,128)(2,1)S(1)}, u32[]{:S(2)}, u32[]{:S(2)}) collective-permute-start(bf16[1024,256]{1,0:T(8,128)(2,1)S(1)} %collective-permute-done.5.refs_13_), channel_id=1, source_target_pairs={{0,4},{1,3},{4,8},{5,1},{8,12},{9,5},{12,14},{13,9},{14,10},{15,13... | collective-permute-start | bytes 1572872 | tf_op jit(solution)/shard_map/ppermute | solution.py:245
  37.3 6.5 %collective-permute-start.13 = (bf16[1024,256]{1,0:T(8,128)(2,1)S(1)}, bf16[1024,256]{1,0:T(8,128)(2,1)S(1)}, u32[]{:S(2)}, u32[]{:S(2)}) collective-permute-start(bf16[1024,256]{1,0:T(8,128)(2,1)S(1)} %collective-permute-done.6.refs_14_), channel_id=1, source_target_pairs={{0,1},{1,0},{2,3},{3,2},{4,5},{5,4},{6,7},{7,6},{8,9},{9,8},{10,11... | collective-permute-start | bytes 1572872 | tf_op jit(solution)/shard_map/ppermute | solution.py:248
  38.2 5.6 %collective-permute-start.14 = (bf16[1024,256]{1,0:T(8,128)(2,1)S(1)}, bf16[1024,256]{1,0:T(8,128)(2,1)S(1)}, u32[]{:S(2)}, u32[]{:S(2)}) collective-permute-start(bf16[1024,256]{1,0:T(8,128)(2,1)S(1)} %collective-permute-done.5.refs_13_), channel_id=1, source_target_pairs={{0,1},{1,0},{2,3},{3,2},{4,5},{5,4},{6,7},{7,6},{8,9},{9,8},{10,11... | collective-permute-start | bytes 1572872 | tf_op jit(solution)/shard_map/ppermute | solution.py:248
  42.9 11.0 %collective-permute-start.8 = (bf16[1024,256]{1,0:T(8,128)(2,1)S(1)}, bf16[1024,256]{1,0:T(8,128)(2,1)S(1)}, u32[]{:S(2)}, u32[]{:S(2)}) collective-permute-start(bf16[1024,256]{1,0:T(8,128)(2,1)S(1)} %collective-permute-done.7.refs_15_), channel_id=1, source_target_pairs={{0,1},{1,0},{2,3},{3,2},{4,5},{5,4},{6,7},{7,6},{8,9},{9,8},{10,11... | collective-permute-start | bytes 1572872 | tf_op jit(solution)/shard_map/ppermute | solution.py:248
  57.7 1.8 %collective-permute-start.15 = (bf16[48,4096]{1,0:T(8,128)(2,1)S(1)}, bf16[48,4096]{1,0:T(8,128)(2,1)S(1)}, u32[]{:S(2)}, u32[]{:S(2)}) collective-permute-start(bf16[48,4096]{1,0:T(8,128)(2,1)S(1)} %get-tuple-element.54), channel_id=1, source_target_pairs={{0,1},{1,0},{2,3},{3,2},{4,5},{5,4},{6,7},{7,6},{8,9},{9,8},{10,11... | collective-permute-start | bytes 1179656 | tf_op jit(solution)/shard_map/ppermute | solution.py:248
where the time goes:
time: 60.4 us
  waiting for transfers between devices  31.5 us (52%)
  Pallas kernels  20.2 us (33%)
  starting transfers between devices  7.07 us (12%)
  other arithmetic  0.93 us (2%)
  local copies, waits for them, and re-layouts  0.68 us (1%)
    ppermute x7, waiting for transfers between devices, send_on(): return lax.ppermute(piece, ('mesh', 'writer'), onward)  28.2 us
    pallas_call x3, Pallas kernels, decode_tiles(): pl.pallas_call(lambda *refs: decode_kernel(stage, blocks, pieces, tiles,...  15.8 us
    ppermute x9, starting transfers between devices, swap(): return lax.ppermute(piece, 'writer', [(0, 1), (1, 0)])  5.49 us
    pallas_call x1, Pallas kernels, prepare(): pl.pallas_call(lambda *refs: prepare_kernel(count, columns, blocks, *refs...  4.34 us
    ppermute x9, waiting for transfers between devices, swap(): return lax.ppermute(piece, 'writer', [(0, 1), (1, 0)])  3.24 us
    ppermute x7, starting transfers between devices, send_on(): return lax.ppermute(piece, ('mesh', 'writer'), onward)  1.58 us
  transfers between devices with their start and end apart: 16, of which 9 were waited for; matrix products, arithmetic and copies ran while one was open for 1% of the time, Pallas kernels for 27%

commit v1 on v0

--- a/solution.py
+++ b/solution.py
@@ -7,8 +7,8 @@
 
 BLK = 128
 K = 4
-GROUP = 4
-META = 8
+GROUP = 8
+META = 5
 
 
 def ring_order(count, columns):
@@ -18,7 +18,7 @@
 
 
 def prepare_kernel(count, columns, blocks, wanted, slots, live, order, w_out, b_out, state, w_in, nodes, interp, *rest):
-    meta, heads, bias, ordered, w_in_kept, nodes_kept, interp_kept, codes, sem = rest
+    meta, heads, bias, ordered, w_in_kept, nodes_kept, interp_kept, entry_stage, sem = rest
     core = lax.axis_index("writer")
     tiles = live.shape[0] // 2
     first_tile = core * tiles
@@ -39,32 +39,37 @@
     here = place(lax.axis_index("mesh"))
     first_stage = stages_of(count)[0]
 
+    listed = wanted.shape[1]
+    entry_work = tiles * META + len(stages_of(count)) * (tiles + 1)
+    for stage in range(len(stages_of(count))):
+        meta[tiles * META + stage * (tiles + 1)] = 0
+        meta[entry_work + stage * (listed + 1)] = 0
+
     def locate(entry, _):
         block = wanted[0, entry]
         behind = here - place(lax.div(block, blocks))
         behind = jnp.where(core == 0, behind, -behind)
         behind = jnp.where(behind < 0, behind + count, behind)
-        codes[entry] = behind * blocks + lax.rem(block, blocks)
+        stage = jnp.maximum(jnp.minimum(behind, count - behind), first_stage) - first_stage
+        entry_stage[entry] = stage
+        work = entry_work + stage * (listed + 1)
+        meta[work] = meta[work] + 1
+        code = behind * blocks + lax.rem(block, blocks)
+        meta[work + meta[work]] = code * listed + entry
         return 0
 
-    lax.fori_loop(0, wanted.shape[1], locate, 0)
-    stages = len(stages_of(count))
-    for stage in range(stages):
-        meta[tiles * META + stage * (tiles + 1)] = 0
+    lax.fori_loop(0, listed, locate, 0)
 
     def describe(tile, _):
         number = first_tile + tile
         alive = live[number]
-        stage = jnp.int32(first_stage)
+        stage = jnp.int32(0)
         for k in range(K):
-            code = codes[slots[k, number]]
-            behind = lax.div(code, blocks)
-            distance = jnp.minimum(behind, count - behind)
-            stage = jnp.where(k < alive, jnp.maximum(stage, distance), stage)
-            meta[tile * META + k] = code
+            entry = slots[jnp.where(k < alive, k, 0), number]
+            stage = jnp.maximum(stage, entry_stage[entry])
+            meta[tile * META + k] = entry
         meta[tile * META + K] = alive
-        meta[tile * META + K + 1] = number
-        work = tiles * META + (stage - first_stage) * (tiles + 1)
+        work = tiles * META + stage * (tiles + 1)
         meta[work] = meta[work] + 1
         meta[work + meta[work]] = tile
         return 0
@@ -104,7 +109,7 @@
     return pl.pallas_call(
         lambda *refs: prepare_kernel(count, columns, blocks, *refs),
         out_shape=[
-            jax.ShapeDtypeStruct((tiles * META + len(stages_of(count)) * (tiles + 1),), jnp.int32),
+            jax.ShapeDtypeStruct((tiles * META + len(stages_of(count)) * (tiles + wanted.shape[1] + 2),), jnp.int32),
             jax.ShapeDtypeStruct((rows, w_out.shape[1]), jnp.bfloat16),
             jax.ShapeDtypeStruct((rows, 1), jnp.float32),
             jax.ShapeDtypeStruct((rows, state.shape[1]), jnp.bfloat16),
@@ -126,27 +131,37 @@
     return list(range(max(far - 2, 1), far + 1))
 
 
-def decode_kernel(stage, blocks, pieces, tiles, held, *refs):
+def decode_kernel(stage, stages, blocks, pieces, tiles, held, *refs):
     meta, w_in, b_in, w_out, b_out, state, interp = refs[:7]
     piece_refs = refs[7 : 7 + 2 * len(pieces)]
-    own_out, other_out, x_buf = refs[7 + held + 2 * len(pieces) :]
+    own_out, other_out, found = refs[7 + held + 2 * len(pieces) :]
     half = piece_refs[0].shape[1]
     rows = own_out.shape[0]
+    listed = found.shape[0]
     core = lax.axis_index("writer")
 
     def columns_of(tile):
         return pl.ds(pl.multiple_of(tile * BLK, BLK), BLK)
 
-    def take_block(code, j, k, low, high):
+    def take_block(code, entry, low, high):
         if high - low > 1:
             middle = (low + high) // 2
             below = code < pieces[middle] * blocks
-            pl.when(below)(lambda: take_block(code, j, k, low, middle))
-            pl.when(jnp.logical_not(below))(lambda: take_block(code, j, k, middle, high))
+            pl.when(below)(lambda: take_block(code, entry, low, middle))
+            pl.when(jnp.logical_not(below))(lambda: take_block(code, entry, middle, high))
             return
         source = pl.ds(pl.multiple_of((code - pieces[low] * blocks) * BLK, BLK), BLK)
         for h in range(2):
-            x_buf[j, k * BLK : (k + 1) * BLK, h * half : (h + 1) * half] = piece_refs[2 * low + h][source, :]
+            found[entry, :, h * half : (h + 1) * half] = piece_refs[2 * low + h][source, :]
+
+    fresh = tiles * META + stages * (tiles + 1) + stage * (listed + 1)
+
+    def take(i, _):
+        packed = meta[fresh + 1 + i]
+        take_block(lax.div(packed, listed), lax.rem(packed, listed), 0, len(pieces))
+        return 0
+
+    lax.fori_loop(0, meta[fresh], take, 0)
 
     work = tiles * META + stage * (tiles + 1)
     count = meta[work]
@@ -154,31 +169,18 @@
     def tile_at(i):
         return meta[work + 1 + i]
 
-    def arrive(i, j):
-        tile = tile_at(i)
-        live = meta[tile * META + K]
-        for k in range(K):
-
-            @pl.when(k < live)
-            def _():
-                take_block(meta[tile * META + k], j, k, 0, len(pieces))
-
-            @pl.when(k >= live)
-            def _():
-                x_buf[j, k * BLK : (k + 1) * BLK, :] = jnp.zeros((BLK, 2 * half), jnp.bfloat16)
-
-    def group(g, _):
-        for j in range(GROUP):
-
-            @pl.when(GROUP * g + j < count)
-            def _():
-                arrive(GROUP * g + j, j)
-
+    def decode(first, size):
         aggregated = []
-        for j in range(GROUP):
-            tile = tile_at(jnp.minimum(GROUP * g + j, count - 1))
-            spread = jnp.concatenate([interp[tile, k] for k in range(K)], axis=1)
-            aggregated.append(jnp.dot(spread, x_buf[j], preferred_element_type=jnp.float32).astype(jnp.bfloat16))
+        for j in range(size):
+            tile = tile_at(jnp.minimum(first + j, count - 1))
+            live = meta[tile * META + K]
+            spread = [interp[tile, k] for k in range(K)]
+            spread = [a if k == 0 else jnp.where(k < live, a, jnp.zeros_like(a)) for k, a in enumerate(spread)]
+            nodes = [found[meta[tile * META + k]] for k in range(K)]
+            total = jnp.dot(
+                jnp.concatenate(spread, axis=1), jnp.concatenate(nodes, axis=0), preferred_element_type=jnp.float32
+            )
+            aggregated.append(total.astype(jnp.bfloat16))
         aggregated = jnp.concatenate(aggregated, axis=0)
         layer = b_in[...].astype(jnp.float32)
         for h in range(2):
@@ -191,8 +193,8 @@
             w_out[...], hidden, (((1,), (1,)), ((), ())), preferred_element_type=jnp.float32
         )
         decoded = decoded + b_out[...]
-        for j in range(GROUP):
-            i = GROUP * g + j
+        for j in range(size):
+            i = first + j
 
             @pl.when(i < count)
             def _():
@@ -202,12 +204,19 @@
                 own_out[:, columns_of(tile)] = after[:rows]
                 other_out[:, columns_of(tile)] = after[rows:]
 
+    def large(g, _):
+        decode(g * GROUP, GROUP)
         return 0
 
-    lax.fori_loop(0, (count + GROUP - 1) // GROUP, group, 0)
-
-
-def decode_tiles(stage, blocks, pieces, tiles, small, arrays, outs):
+    groups = (count + GROUP // 2 - 1) // GROUP
+    lax.fori_loop(0, groups, large, 0)
+
+    @pl.when(groups * GROUP < count)
+    def _():
+        decode(groups * GROUP, GROUP // 2)
+
+
+def decode_tiles(stage, stages, blocks, pieces, tiles, listed, small, arrays, outs):
     flat = [half for pair in arrays for half in pair]
     half = flat[0].shape[1]
     state = small[-2]
@@ -216,12 +225,12 @@
     first_out = 7 + len(flat)
     share = max(tiles // 4, 1)
     return pl.pallas_call(
-        lambda *refs: decode_kernel(stage, blocks, pieces, tiles, len(outs), *refs),
-        out_shape=[jax.ShapeDtypeStruct((rows, state.shape[1]), jnp.bfloat16)] * 2,
+        lambda *refs: decode_kernel(stage, stages, blocks, pieces, tiles, len(outs), *refs),
+        out_shape=[jax.ShapeDtypeStruct((rows, state.shape[1]), jnp.bfloat16)] * 2
+        + [jax.ShapeDtypeStruct((listed, BLK, 2 * half), jnp.bfloat16)],
         in_specs=[pl.BlockSpec(memory_space=pltpu.SMEM)] + [vmem] * (6 + len(flat) + len(outs)),
-        out_specs=[vmem] * 2,
+        out_specs=[vmem] * 3,
         input_output_aliases={first_out + j: j for j in range(len(outs))},
-        scratch_shapes=[pltpu.VMEM((GROUP, K * BLK, 2 * half), jnp.bfloat16)],
         compiler_params=pltpu.CompilerParams(vmem_limit_bytes=16 * 2**20),
         cost_estimate=pl.CostEstimate(
             flops=share * BLK * 2 * (K * BLK * 2 * half + 4 * half * half + 4 * half * rows),
@@ -288,9 +297,20 @@
         same, cross = [mesh_nodes], [other_nodes]
         table = {0: (nodes_kept, other_nodes)}
         def decode(d, outs):
-            pieces = [p for p in sorted(table) if min(p, count - p) <= d]
+            distances = range(d + 1) if d == stages[0] else (d,)
+            pieces = [p for p in sorted(table) if min(p, count - p) in distances]
             return list(
-                decode_tiles(stages.index(d), blocks, pieces, tiles, small, [table[p] for p in pieces], outs)
+                decode_tiles(
+                    stages.index(d),
+                    len(stages),
+                    blocks,
+                    pieces,
+                    tiles,
+                    wanted.shape[1],
+                    small,
+                    [table[p] for p in pieces],
+                    outs,
+                )
             )
 
         for d in range(1, far + 1):

time: 60.4 us -> 55.4 us (0.917)
  the two profiles are of different devices: /device:TPU:29 before, /device:TPU:0 now
where the time goes in v1:
time: 55.4 us; the launch traced here: 54.9 us
  waiting for transfers between devices  19.6 us (35%)
  Pallas kernels  16.8 us (30%)
  starting transfers between devices  16.7 us (30%)
  other arithmetic  0.93 us (2%)
  local copies, waits for them, and re-layouts  0.68 us (1%)
    ppermute x7, waiting for transfers between devices, send_on(): return lax.ppermute(piece, ('mesh', 'writer'), onward)  17.9 us
    ppermute x7, starting transfers between devices, send_on(): return lax.ppermute(piece, ('mesh', 'writer'), onward)  15.1 us
    pallas_call x3, Pallas kernels, decode_tiles(): pl.pallas_call(lambda *refs: decode_kernel(stage, stages, blocks, pieces,...  12.3 us
    pallas_call x1, Pallas kernels, prepare(): pl.pallas_call(lambda *refs: prepare_kernel(count, columns, blocks, *refs...  4.51 us
    ppermute x9, waiting for transfers between devices, swap(): return lax.ppermute(piece, 'writer', [(0, 1), (1, 0)])  1.73 us
    ppermute x9, starting transfers between devices, swap(): return lax.ppermute(piece, 'writer', [(0, 1), (1, 0)])  1.62 us
  transfers between devices with their start and end apart: 16, of which 6 were waited for; matrix products, arithmetic and copies ran while one was open for 1% of the time, Pallas kernels for 24%

profile of v1, /device:TPU:0, one launch (start us, length us, event | category | flops | bytes accessed | tf_op | source)
XLA Modules:
  0.0 54.9 jit_solution(17343775000418422151)
XLA Ops:
  0.0 0.5 collective-permute-start.5
  0.5 2.6 %collective-permute-start = (bf16[1024,256]{1,0:T(8,128)(2,1)}, bf16[1024,256]{1,0:T(8,128)(2,1)S(1)}, u32[]{:S(2)}, u32[]{:S(2)}) collective-permute-start(bf16[1024,256]{1,0:T(8,128)(2,1)} %refs_8_.1), channel_id=1, source_target_pairs={{0,4},{1,3},{4,8},{5,1},{8,12},{9,5},{12,14},{13,9},{14,10},{15,13... | collective-permute-start | bytes 1572872 | tf_op jit(solution)/shard_map/ppermute | solution.py:254
  3.0 0.0 collective-permute-done.5.refs_8_
  3.0 2.1 %collective-permute-start.6 = (bf16[1024,256]{1,0:T(8,128)(2,1)S(1)}, bf16[1024,256]{1,0:T(8,128)(2,1)S(1)}, u32[]{:S(2)}, u32[]{:S(2)}) collective-permute-start(bf16[1024,256]{1,0:T(8,128)(2,1)S(1)} %collective-permute-done.5.refs_8_), channel_id=1, source_target_pairs={{0,4},{1,3},{4,8},{5,1},{8,12},{9,5},{12,14},{13,9},{14,10},{15,13... | collective-permute-start | bytes 1572872 | tf_op jit(solution)/shard_map/ppermute | solution.py:254
  5.1 0.7 %broadcast_in_dim.11.refs_2_ = bf16[1,512]{1,0:T(2,128)(2,1)S(1)} reshape(bf16[512]{0:T(512)(128)(2,1)} %param.18) | data formatting | bytes 2048 | tf_op jit(solution)/shard_map/broadcast_in_dim | solution.py:293
  5.8 4.5 %prepare.1 = (s32[358]{0:T(512)S(1)}, bf16[96,512]{1,0:T(8,128)(2,1)S(1)}, f32[96,1]{1,0:T(8,128)S(1)}, bf16[96,4096]{1,0:T(8,128)(2,1)S(1)}, bf16[512,512]{1,0:...) custom-call(s32[1,32]{1,0:T(1,128)} %refs_0_.1, s32[4,64]{1,0:T(4,128)} %bitcast.5, ...), custom_call_target="tpu_custom_call" | custom-call | flops 62914560 | bytes 1966080 | tf_op jit(solution)/shard_map/prepare/pallas_call | solution.py:109
  10.3 0.0 collective-permute-done.refs_9_
  10.4 2.1 %collective-permute-start.1 = (bf16[1024,256]{1,0:T(8,128)(2,1)S(1)}, bf16[1024,256]{1,0:T(8,128)(2,1)S(1)}, u32[]{:S(2)}, u32[]{:S(2)}) collective-permute-start(bf16[1024,256]{1,0:T(8,128)(2,1)S(1)} %collective-permute-done.refs_9_), channel_id=1, source_target_pairs={{0,4},{1,3},{4,8},{5,1},{8,12},{9,5},{12,14},{13,9},{14,10},{15,13... | collective-permute-start | bytes 1572872 | tf_op jit(solution)/shard_map/ppermute | solution.py:254
  12.4 3.5 %collective-permute-done.6.refs_10_ = bf16[1024,256]{1,0:T(8,128)(2,1)S(1)} collective-permute-done((bf16[1024,256]{1,0:T(8,128)(2,1)S(1)}, bf16[1024,256]{1,0:T(8,128)(2,1)S(1)}, u32[]{:S(2)}, u32[]{:S(2)}) %collective-permute-start.6) | collective-permute-done | bytes 524320 | tf_op jit(solution)/shard_map/ppermute | solution.py:254
  16.0 2.1 %collective-permute-start.7 = (bf16[1024,256]{1,0:T(8,128)(2,1)S(1)}, bf16[1024,256]{1,0:T(8,128)(2,1)S(1)}, u32[]{:S(2)}, u32[]{:S(2)}) collective-permute-start(bf16[1024,256]{1,0:T(8,128)(2,1)S(1)} %collective-permute-done.6.refs_10_), channel_id=1, source_target_pairs={{0,4},{1,3},{4,8},{5,1},{8,12},{9,5},{12,14},{13,9},{14,10},{15,13... | collective-permute-start | bytes 1572872 | tf_op jit(solution)/shard_map/ppermute | solution.py:254
  18.0 0.0 collective-permute-start.12
  18.0 3.5 %collective-permute-done.1.refs_11_ = bf16[1024,256]{1,0:T(8,128)(2,1)S(1)} collective-permute-done((bf16[1024,256]{1,0:T(8,128)(2,1)S(1)}, bf16[1024,256]{1,0:T(8,128)(2,1)S(1)}, u32[]{:S(2)}, u32[]{:S(2)}) %collective-permute-start.1) | collective-permute-done | bytes 524320 | tf_op jit(solution)/shard_map/ppermute | solution.py:254
  21.6 2.1 %collective-permute-start.2 = (bf16[1024,256]{1,0:T(8,128)(2,1)S(1)}, bf16[1024,256]{1,0:T(8,128)(2,1)S(1)}, u32[]{:S(2)}, u32[]{:S(2)}) collective-permute-start(bf16[1024,256]{1,0:T(8,128)(2,1)S(1)} %collective-permute-done.1.refs_11_), channel_id=1, source_target_pairs={{0,4},{1,3},{4,8},{5,1},{8,12},{9,5},{12,14},{13,9},{14,10},{15,13... | collective-permute-start | bytes 1572872 | tf_op jit(solution)/shard_map/ppermute | solution.py:254
  23.7 0.0 collective-permute-start.10
  23.7 0.5 collective-permute-start.11
  24.2 3.0 %collective-permute-done.7.refs_12_ = bf16[1024,256]{1,0:T(8,128)(2,1)S(1)} collective-permute-done((bf16[1024,256]{1,0:T(8,128)(2,1)S(1)}, bf16[1024,256]{1,0:T(8,128)(2,1)S(1)}, u32[]{:S(2)}, u32[]{:S(2)}) %collective-permute-start.7) | collective-permute-done | bytes 524320 | tf_op jit(solution)/shard_map/ppermute | solution.py:254
  27.2 0.0 collective-permute-start.9
  27.2 0.0 collective-permute-done.12.refs_16_
  27.2 2.1 %collective-permute-start.8 = (bf16[1024,256]{1,0:T(8,128)(2,1)S(1)}, bf16[1024,256]{1,0:T(8,128)(2,1)S(1)}, u32[]{:S(2)}, u32[]{:S(2)}) collective-permute-start(bf16[1024,256]{1,0:T(8,128)(2,1)S(1)} %collective-permute-done.7.refs_12_), channel_id=1, source_target_pairs={{0,4},{1,3},{4,8},{5,1},{8,12},{9,5},{12,14},{13,9},{14,10},{15,13... | collective-permute-start | bytes 1572872 | tf_op jit(solution)/shard_map/ppermute | solution.py:254
  29.3 3.5 %collective-permute-done.2.refs_7_ = bf16[1024,256]{1,0:T(8,128)(2,1)S(1)} collective-permute-done((bf16[1024,256]{1,0:T(8,128)(2,1)S(1)}, bf16[1024,256]{1,0:T(8,128)(2,1)S(1)}, u32[]{:S(2)}, u32[]{:S(2)}) %collective-permute-start.2) | collective-permute-done | bytes 524320 | tf_op jit(solution)/shard_map/ppermute | solution.py:254
  32.8 2.1 %collective-permute-start.3 = (bf16[1024,256]{1,0:T(8,128)(2,1)S(1)}, bf16[1024,256]{1,0:T(8,128)(2,1)S(1)}, u32[]{:S(2)}, u32[]{:S(2)}) collective-permute-start(bf16[1024,256]{1,0:T(8,128)(2,1)S(1)} %collective-permute-done.2.refs_7_), channel_id=1, source_target_pairs={{0,4},{1,3},{4,8},{5,1},{8,12},{9,5},{12,14},{13,9},{14,10},{15,13... | collective-permute-start | bytes 1572872 | tf_op jit(solution)/shard_map/ppermute | solution.py:254
  34.9 0.0 collective-permute-done.10.refs_14_
  34.9 0.0 collective-permute-done.11.refs_15_
  34.9 0.0 collective-permute-done.9.refs_13_
  34.9 4.3 %decode_tiles.3 = (bf16[48,4096]{1,0:T(8,128)(2,1)S(1)}, bf16[48,4096]{1,0:T(8,128)(2,1)S(1)}, bf16[32,128,512]{2,1,0:T(8,128)(2,1)S(1)}) custom-call(s32[358]{0:T(512)S(1)} %get-tuple-element.39.refs_0_, bf16[512,512]{1,0:T(8,128)(2,1)S(1)} %get-tuple-element.40.refs_1_, bf16[1,512]{1,0:T(2,128)(2,1)S(1)} %broadcast_in_dim.11.refs_2_, ...), custom_call_target="tpu_custom_call" | custom-call | flops 1174405120 | bytes 7864320 | tf_op jit(solution)/shard_map/decode_tiles/pallas_call | solution.py:227
  39.2 0.0 collective-permute-done.8.refs_8_
  39.2 0.2 collective-permute-start.13
  39.4 0.4 collective-permute-start.14
  39.8 4.3 %collective-permute-done.3.refs_7_ = bf16[1024,256]{1,0:T(8,128)(2,1)S(1)} collective-permute-done((bf16[1024,256]{1,0:T(8,128)(2,1)S(1)}, bf16[1024,256]{1,0:T(8,128)(2,1)S(1)}, u32[]{:S(2)}, u32[]{:S(2)}) %collective-permute-start.3) | collective-permute-done | bytes 524320 | tf_op jit(solution)/shard_map/ppermute | solution.py:254
  44.0 0.0 collective-permute-start.4
  44.0 0.0 collective-permute-done.13.refs_9_
  44.1 0.0 collective-permute-done.14.refs_10_
  44.1 4.5 %decode_tiles.4 = (bf16[48,4096]{1,0:T(8,128)(2,1)S(1)}, bf16[48,4096]{1,0:T(8,128)(2,1)S(1)}, bf16[32,128,512]{2,1,0:T(8,128)(2,1)S(1)}) custom-call(s32[358]{0:T(512)S(1)} %get-tuple-element.39.refs_0_, bf16[512,512]{1,0:T(8,128)(2,1)S(1)} %get-tuple-element.40.refs_1_, ...), custom_call_target="tpu_custom_call", output_to_operand_aliasing={{0}: (11, {}), {1}: (12, {}), {2}: (13, {})} | custom-call | flops 1174405120 | bytes 7864320 | tf_op jit(solution)/shard_map/decode_tiles/pallas_call | solution.py:227
  48.5 0.0 collective-permute-done.4.refs_8_
  48.6 3.6 %decode_tiles.5 = (bf16[48,4096]{1,0:T(8,128)(2,1)S(1)}, bf16[48,4096]{1,0:T(8,128)(2,1)S(1)}, bf16[32,128,512]{2,1,0:T(8,128)(2,1)S(1)}) custom-call(s32[358]{0:T(512)S(1)} %get-tuple-element.39.refs_0_, bf16[512,512]{1,0:T(8,128)(2,1)S(1)} %get-tuple-element.40.refs_1_, ...), custom_call_target="tpu_custom_call", output_to_operand_aliasing={{0}: (9, {}), {1}: (10, {}), {2}: (11, {})} | custom-call | flops 1174405120 | bytes 7864320 | tf_op jit(solution)/shard_map/decode_tiles/pallas_call | solution.py:227
  52.1 0.1 collective-permute-start.15
  52.2 1.7 %collective-permute-done.15 = bf16[48,4096]{1,0:T(8,128)(2,1)S(1)} collective-permute-done((bf16[48,4096]{1,0:T(8,128)(2,1)S(1)}, bf16[48,4096]{1,0:T(8,128)(2,1)S(1)}, u32[]{:S(2)}, u32[]{:S(2)}) %collective-permute-start.15) | collective-permute-done | bytes 393248 | tf_op jit(solution)/shard_map/ppermute | solution.py:257
  54.0 0.9 %pad_maximum_fusion = bf16[40,8192]{1,0:T(8,128)(2,1)} fusion(bf16[40,4096]{1,0:T(8,128)(2,1)S(1)} %get-tuple-element.62, bf16[40,4096]{1,0:T(8,128)(2,1)S(1)} %get-tuple-element.61), kind=kLoop, calls=%fused_computation | loop fusion | flops 1310720 | bytes 1310720 | tf_op jit(solution)/shard_map/concatenate | solution.py:335
  (1 shorter events, 0.0 us)
Async XLA Ops:
  0.0 3.0 %collective-permute-start.5 = (bf16[1024,256]{1,0:T(8,128)(2,1)}, bf16[1024,256]{1,0:T(8,128)(2,1)S(1)}, u32[]{:S(2)}, u32[]{:S(2)}) collective-permute-start(bf16[1024,256]{1,0:T(8,128)(2,1)} %refs_8_.1), channel_id=1, source_target_pairs={{0,1},{1,0},{2,3},{3,2},{4,5},{5,4},{6,7},{7,6},{8,9},{9,8},{10,11... | collective-permute-start | bytes 1572872 | tf_op jit(solution)/shard_map/ppermute | solution.py:257
  0.5 9.9 %collective-permute-start = (bf16[1024,256]{1,0:T(8,128)(2,1)}, bf16[1024,256]{1,0:T(8,128)(2,1)S(1)}, u32[]{:S(2)}, u32[]{:S(2)}) collective-permute-start(bf16[1024,256]{1,0:T(8,128)(2,1)} %refs_8_.1), channel_id=1, source_target_pairs={{0,4},{1,3},{4,8},{5,1},{8,12},{9,5},{12,14},{13,9},{14,10},{15,13... | collective-permute-start | bytes 1572872 | tf_op jit(solution)/shard_map/ppermute | solution.py:254
  3.0 12.9 %collective-permute-start.6 = (bf16[1024,256]{1,0:T(8,128)(2,1)S(1)}, bf16[1024,256]{1,0:T(8,128)(2,1)S(1)}, u32[]{:S(2)}, u32[]{:S(2)}) collective-permute-start(bf16[1024,256]{1,0:T(8,128)(2,1)S(1)} %collective-permute-done.5.refs_8_), channel_id=1, source_target_pairs={{0,4},{1,3},{4,8},{5,1},{8,12},{9,5},{12,14},{13,9},{14,10},{15,13... | collective-permute-start | bytes 1572872 | tf_op jit(solution)/shard_map/ppermute | solution.py:254
  10.4 11.2 %collective-permute-start.1 = (bf16[1024,256]{1,0:T(8,128)(2,1)S(1)}, bf16[1024,256]{1,0:T(8,128)(2,1)S(1)}, u32[]{:S(2)}, u32[]{:S(2)}) collective-permute-start(bf16[1024,256]{1,0:T(8,128)(2,1)S(1)} %collective-permute-done.refs_9_), channel_id=1, source_target_pairs={{0,4},{1,3},{4,8},{5,1},{8,12},{9,5},{12,14},{13,9},{14,10},{15,13... | collective-permute-start | bytes 1572872 | tf_op jit(solution)/shard_map/ppermute | solution.py:254
  16.0 11.2 %collective-permute-start.7 = (bf16[1024,256]{1,0:T(8,128)(2,1)S(1)}, bf16[1024,256]{1,0:T(8,128)(2,1)S(1)}, u32[]{:S(2)}, u32[]{:S(2)}) collective-permute-start(bf16[1024,256]{1,0:T(8,128)(2,1)S(1)} %collective-permute-done.6.refs_10_), channel_id=1, source_target_pairs={{0,4},{1,3},{4,8},{5,1},{8,12},{9,5},{12,14},{13,9},{14,10},{15,13... | collective-permute-start | bytes 1572872 | tf_op jit(solution)/shard_map/ppermute | solution.py:254
  18.0 9.2 %collective-permute-start.12 = (bf16[1024,256]{1,0:T(8,128)(2,1)S(1)}, bf16[1024,256]{1,0:T(8,128)(2,1)S(1)}, u32[]{:S(2)}, u32[]{:S(2)}) collective-permute-start(bf16[1024,256]{1,0:T(8,128)(2,1)S(1)} %collective-permute-done.refs_9_), channel_id=1, source_target_pairs={{0,1},{1,0},{2,3},{3,2},{4,5},{5,4},{6,7},{7,6},{8,9},{9,8},{10,11... | collective-permute-start | bytes 1572872 | tf_op jit(solution)/shard_map/ppermute | solution.py:257
  21.6 11.2 %collective-permute-start.2 = (bf16[1024,256]{1,0:T(8,128)(2,1)S(1)}, bf16[1024,256]{1,0:T(8,128)(2,1)S(1)}, u32[]{:S(2)}, u32[]{:S(2)}) collective-permute-start(bf16[1024,256]{1,0:T(8,128)(2,1)S(1)} %collective-permute-done.1.refs_11_), channel_id=1, source_target_pairs={{0,4},{1,3},{4,8},{5,1},{8,12},{9,5},{12,14},{13,9},{14,10},{15,13... | collective-permute-start | bytes 1572872 | tf_op jit(solution)/shard_map/ppermute | solution.py:254
  23.7 11.2 %collective-permute-start.10 = (bf16[1024,256]{1,0:T(8,128)(2,1)S(1)}, bf16[1024,256]{1,0:T(8,128)(2,1)S(1)}, u32[]{:S(2)}, u32[]{:S(2)}) collective-permute-start(bf16[1024,256]{1,0:T(8,128)(2,1)S(1)} %collective-permute-done.1.refs_11_), channel_id=1, source_target_pairs={{0,1},{1,0},{2,3},{3,2},{4,5},{5,4},{6,7},{7,6},{8,9},{9,8},{10,11... | collective-permute-start | bytes 1572872 | tf_op jit(solution)/shard_map/ppermute | solution.py:257
  23.7 11.2 %collective-permute-start.11 = (bf16[1024,256]{1,0:T(8,128)(2,1)S(1)}, bf16[1024,256]{1,0:T(8,128)(2,1)S(1)}, u32[]{:S(2)}, u32[]{:S(2)}) collective-permute-start(bf16[1024,256]{1,0:T(8,128)(2,1)S(1)} %collective-permute-done.6.refs_10_), channel_id=1, source_target_pairs={{0,1},{1,0},{2,3},{3,2},{4,5},{5,4},{6,7},{7,6},{8,9},{9,8},{10,11... | collective-permute-start | bytes 1572872 | tf_op jit(solution)/shard_map/ppermute | solution.py:257
  27.2 7.7 %collective-permute-start.9 = (bf16[1024,256]{1,0:T(8,128)(2,1)S(1)}, bf16[1024,256]{1,0:T(8,128)(2,1)S(1)}, u32[]{:S(2)}, u32[]{:S(2)}) collective-permute-start(bf16[1024,256]{1,0:T(8,128)(2,1)S(1)} %collective-permute-done.7.refs_12_), channel_id=1, source_target_pairs={{0,1},{1,0},{2,3},{3,2},{4,5},{5,4},{6,7},{7,6},{8,9},{9,8},{10,11... | collective-permute-start | bytes 1572872 | tf_op jit(solution)/shard_map/ppermute | solution.py:257
  27.2 12.0 %collective-permute-start.8 = (bf16[1024,256]{1,0:T(8,128)(2,1)S(1)}, bf16[1024,256]{1,0:T(8,128)(2,1)S(1)}, u32[]{:S(2)}, u32[]{:S(2)}) collective-permute-start(bf16[1024,256]{1,0:T(8,128)(2,1)S(1)} %collective-permute-done.7.refs_12_), channel_id=1, source_target_pairs={{0,4},{1,3},{4,8},{5,1},{8,12},{9,5},{12,14},{13,9},{14,10},{15,13... | collective-permute-start | bytes 1572872 | tf_op jit(solution)/shard_map/ppermute | solution.py:254
  32.8 11.2 %collective-permute-start.3 = (bf16[1024,256]{1,0:T(8,128)(2,1)S(1)}, bf16[1024,256]{1,0:T(8,128)(2,1)S(1)}, u32[]{:S(2)}, u32[]{:S(2)}) collective-permute-start(bf16[1024,256]{1,0:T(8,128)(2,1)S(1)} %collective-permute-done.2.refs_7_), channel_id=1, source_target_pairs={{0,4},{1,3},{4,8},{5,1},{8,12},{9,5},{12,14},{13,9},{14,10},{15,13... | collective-permute-start | bytes 1572872 | tf_op jit(solution)/shard_map/ppermute | solution.py:254
  39.2 4.9 %collective-permute-start.13 = (bf16[1024,256]{1,0:T(8,128)(2,1)S(1)}, bf16[1024,256]{1,0:T(8,128)(2,1)S(1)}, u32[]{:S(2)}, u32[]{:S(2)}) collective-permute-start(bf16[1024,256]{1,0:T(8,128)(2,1)S(1)} %collective-permute-done.8.refs_8_), channel_id=1, source_target_pairs={{0,1},{1,0},{2,3},{3,2},{4,5},{5,4},{6,7},{7,6},{8,9},{9,8},{10,11... | collective-permute-start | bytes 1572872 | tf_op jit(solution)/shard_map/ppermute | solution.py:257
  39.4 4.7 %collective-permute-start.14 = (bf16[1024,256]{1,0:T(8,128)(2,1)S(1)}, bf16[1024,256]{1,0:T(8,128)(2,1)S(1)}, u32[]{:S(2)}, u32[]{:S(2)}) collective-permute-start(bf16[1024,256]{1,0:T(8,128)(2,1)S(1)} %collective-permute-done.2.refs_7_), channel_id=1, source_target_pairs={{0,1},{1,0},{2,3},{3,2},{4,5},{5,4},{6,7},{7,6},{8,9},{9,8},{10,11... | collective-permute-start | bytes 1572872 | tf_op jit(solution)/shard_map/ppermute | solution.py:257
  44.0 4.5 %collective-permute-start.4 = (bf16[1024,256]{1,0:T(8,128)(2,1)S(1)}, bf16[1024,256]{1,0:T(8,128)(2,1)S(1)}, u32[]{:S(2)}, u32[]{:S(2)}) collective-permute-start(bf16[1024,256]{1,0:T(8,128)(2,1)S(1)} %collective-permute-done.3.refs_7_), channel_id=1, source_target_pairs={{0,1},{1,0},{2,3},{3,2},{4,5},{5,4},{6,7},{7,6},{8,9},{9,8},{10,11... | collective-permute-start | bytes 1572872 | tf_op jit(solution)/shard_map/ppermute | solution.py:257
  52.1 1.8 %collective-permute-start.15 = (bf16[48,4096]{1,0:T(8,128)(2,1)S(1)}, bf16[48,4096]{1,0:T(8,128)(2,1)S(1)}, u32[]{:S(2)}, u32[]{:S(2)}) collective-permute-start(bf16[48,4096]{1,0:T(8,128)(2,1)S(1)} %get-tuple-element.60), channel_id=1, source_target_pairs={{0,1},{1,0},{2,3},{3,2},{4,5},{5,4},{6,7},{7,6},{8,9},{9,8},{10,11... | collective-permute-start | bytes 1179656 | tf_op jit(solution)/shard_map/ppermute | solution.py:257

commit v2 on v1

--- a/solution.py
+++ b/solution.py
@@ -128,7 +128,7 @@
 
 def stages_of(count):
     far = count // 2
-    return list(range(max(far - 2, 1), far + 1))
+    return list(range(max(far - 3, 1), far + 1))
 
 
 def decode_kernel(stage, stages, blocks, pieces, tiles, held, *refs):
@@ -194,15 +194,11 @@
         )
         decoded = decoded + b_out[...]
         for j in range(size):
-            i = first + j
-
-            @pl.when(i < count)
-            def _():
-                tile = tile_at(i)
-                before = state[:, columns_of(tile)].astype(jnp.float32)
-                after = (before + decoded[:, j * BLK : (j + 1) * BLK]).astype(jnp.bfloat16)
-                own_out[:, columns_of(tile)] = after[:rows]
-                other_out[:, columns_of(tile)] = after[rows:]
+            tile = tile_at(jnp.minimum(first + j, count - 1))
+            before = state[:, columns_of(tile)].astype(jnp.float32)
+            after = (before + decoded[:, j * BLK : (j + 1) * BLK]).astype(jnp.bfloat16)
+            own_out[:, columns_of(tile)] = after[:rows]
+            other_out[:, columns_of(tile)] = after[rows:]
 
     def large(g, _):
         decode(g * GROUP, GROUP)

time: 55.4 us -> 55.2 us (level)
  starting transfers between devices: 16.7 us -> 18.8 us
  waiting for transfers between devices: 19.6 us -> 18.5 us
  Pallas kernels: 16.8 us -> 15.8 us
    ppermute x9, starting transfers between devices: 1.62 us -> 3.77 us  [swap(): return lax.ppermute(piece, 'writer', [(0, 1), (1, 0)])]
    pallas_call x3 -> x4, Pallas kernels: 12.3 us -> 11.2 us  [decode_tiles(): pl.pallas_call(lambda *refs: decode_kernel(stage, stages, blocks, pieces,...]
    ppermute x7, waiting for transfers between devices: 17.9 us -> 17.1 us  [send_on(): return lax.ppermute(piece, ('mesh', 'writer'), onward)]
  transfers between devices with their start and end apart: 16 -> 16, of which waited for: 6 -> 7; matrix products, arithmetic and copies ran while one was open for 1% -> 1% of each run, Pallas kernels for 24% -> 21%
where the time goes in v2:
time: 55.2 us; the launch traced here: 54.7 us
  starting transfers between devices  18.8 us (34%)
  waiting for transfers between devices  18.5 us (34%)
  Pallas kernels  15.8 us (29%)
  other arithmetic  0.93 us (2%)
  local copies, waits for them, and re-layouts  0.68 us (1%)
    ppermute x7, waiting for transfers between devices, send_on(): return lax.ppermute(piece, ('mesh', 'writer'), onward)  17.1 us
    ppermute x7, starting transfers between devices, send_on(): return lax.ppermute(piece, ('mesh', 'writer'), onward)  15.1 us
    pallas_call x4, Pallas kernels, decode_tiles(): pl.pallas_call(lambda *refs: decode_kernel(stage, stages, blocks, pieces,...  11.2 us
    pallas_call x1, Pallas kernels, prepare(): pl.pallas_call(lambda *refs: prepare_kernel(count, columns, blocks, *refs...  4.52 us
    ppermute x9, starting transfers between devices, swap(): return lax.ppermute(piece, 'writer', [(0, 1), (1, 0)])  3.77 us
    ppermute x9, waiting for transfers between devices, swap(): return lax.ppermute(piece, 'writer', [(0, 1), (1, 0)])  1.41 us
  transfers between devices with their start and end apart: 16, of which 7 were waited for; matrix products, arithmetic and copies ran while one was open for 1% of the time, Pallas kernels for 21%

profile of v2, /device:TPU:0, one launch (start us, length us, event | category | flops | bytes accessed | tf_op | source)
XLA Modules:
  0.0 54.7 jit_solution(3697039498742687136)
XLA Ops:
  0.0 0.5 collective-permute-start.5
  0.5 2.6 %collective-permute-start = (bf16[1024,256]{1,0:T(8,128)(2,1)}, bf16[1024,256]{1,0:T(8,128)(2,1)S(1)}, u32[]{:S(2)}, u32[]{:S(2)}) collective-permute-start(bf16[1024,256]{1,0:T(8,128)(2,1)} %refs_8_.1), channel_id=1, source_target_pairs={{0,4},{1,3},{4,8},{5,1},{8,12},{9,5},{12,14},{13,9},{14,10},{15,13... | collective-permute-start | bytes 1572872 | tf_op jit(solution)/shard_map/ppermute | solution.py:250
  3.0 0.0 collective-permute-done.5.refs_8_
  3.0 2.1 %collective-permute-start.6 = (bf16[1024,256]{1,0:T(8,128)(2,1)S(1)}, bf16[1024,256]{1,0:T(8,128)(2,1)S(1)}, u32[]{:S(2)}, u32[]{:S(2)}) collective-permute-start(bf16[1024,256]{1,0:T(8,128)(2,1)S(1)} %collective-permute-done.5.refs_8_), channel_id=1, source_target_pairs={{0,4},{1,3},{4,8},{5,1},{8,12},{9,5},{12,14},{13,9},{14,10},{15,13... | collective-permute-start | bytes 1572872 | tf_op jit(solution)/shard_map/ppermute | solution.py:250
  5.1 0.7 %broadcast_in_dim.11.refs_2_ = bf16[1,512]{1,0:T(2,128)(2,1)S(1)} reshape(bf16[512]{0:T(512)(128)(2,1)} %param.18) | data formatting | bytes 2048 | tf_op jit(solution)/shard_map/broadcast_in_dim | solution.py:289
  5.8 4.5 %prepare.1 = (s32[424]{0:T(512)S(1)}, bf16[96,512]{1,0:T(8,128)(2,1)S(1)}, f32[96,1]{1,0:T(8,128)S(1)}, bf16[96,4096]{1,0:T(8,128)(2,1)S(1)}, bf16[512,512]{1,0:...) custom-call(s32[1,32]{1,0:T(1,128)} %refs_0_.1, s32[4,64]{1,0:T(4,128)} %bitcast.5, ...), custom_call_target="tpu_custom_call" | custom-call | flops 62914560 | bytes 1966080 | tf_op jit(solution)/shard_map/prepare/pallas_call | solution.py:109
  10.4 0.0 collective-permute-done.refs_9_
  10.4 2.0 %collective-permute-start.1 = (bf16[1024,256]{1,0:T(8,128)(2,1)S(1)}, bf16[1024,256]{1,0:T(8,128)(2,1)S(1)}, u32[]{:S(2)}, u32[]{:S(2)}) collective-permute-start(bf16[1024,256]{1,0:T(8,128)(2,1)S(1)} %collective-permute-done.refs_9_), channel_id=1, source_target_pairs={{0,4},{1,3},{4,8},{5,1},{8,12},{9,5},{12,14},{13,9},{14,10},{15,13... | collective-permute-start | bytes 1572872 | tf_op jit(solution)/shard_map/ppermute | solution.py:250
  12.4 0.0 collective-permute-start.10
  12.4 3.5 %collective-permute-done.6.refs_10_ = bf16[1024,256]{1,0:T(8,128)(2,1)S(1)} collective-permute-done((bf16[1024,256]{1,0:T(8,128)(2,1)S(1)}, bf16[1024,256]{1,0:T(8,128)(2,1)S(1)}, u32[]{:S(2)}, u32[]{:S(2)}) %collective-permute-start.6) | collective-permute-done | bytes 524320 | tf_op jit(solution)/shard_map/ppermute | solution.py:250
  16.0 0.0 collective-permute-start.9
  16.0 2.1 %collective-permute-start.7 = (bf16[1024,256]{1,0:T(8,128)(2,1)S(1)}, bf16[1024,256]{1,0:T(8,128)(2,1)S(1)}, u32[]{:S(2)}, u32[]{:S(2)}) collective-permute-start(bf16[1024,256]{1,0:T(8,128)(2,1)S(1)} %collective-permute-done.6.refs_10_), channel_id=1, source_target_pairs={{0,4},{1,3},{4,8},{5,1},{8,12},{9,5},{12,14},{13,9},{14,10},{15,13... | collective-permute-start | bytes 1572872 | tf_op jit(solution)/shard_map/ppermute | solution.py:250
  18.0 3.5 %collective-permute-done.1.refs_7_ = bf16[1024,256]{1,0:T(8,128)(2,1)S(1)} collective-permute-done((bf16[1024,256]{1,0:T(8,128)(2,1)S(1)}, bf16[1024,256]{1,0:T(8,128)(2,1)S(1)}, u32[]{:S(2)}, u32[]{:S(2)}) %collective-permute-start.1) | collective-permute-done | bytes 524320 | tf_op jit(solution)/shard_map/ppermute | solution.py:250
  21.6 2.1 %collective-permute-start.2 = (bf16[1024,256]{1,0:T(8,128)(2,1)S(1)}, bf16[1024,256]{1,0:T(8,128)(2,1)S(1)}, u32[]{:S(2)}, u32[]{:S(2)}) collective-permute-start(bf16[1024,256]{1,0:T(8,128)(2,1)S(1)} %collective-permute-done.1.refs_7_), channel_id=1, source_target_pairs={{0,4},{1,3},{4,8},{5,1},{8,12},{9,5},{12,14},{13,9},{14,10},{15,13... | collective-permute-start | bytes 1572872 | tf_op jit(solution)/shard_map/ppermute | solution.py:250
  23.7 0.0 collective-permute-done.10.refs_12_
  23.7 0.0 collective-permute-done.9.refs_11_
  23.7 2.7 %decode_tiles.4 = (bf16[48,4096]{1,0:T(8,128)(2,1)S(1)}, bf16[48,4096]{1,0:T(8,128)(2,1)S(1)}, bf16[32,128,512]{2,1,0:T(8,128)(2,1)S(1)}) custom-call(s32[424]{0:T(512)S(1)} %get-tuple-element.47.refs_0_, bf16[512,512]{1,0:T(8,128)(2,1)S(1)} %get-tuple-element.48.refs_1_, bf16[1,512]{1,0:T(2,128)(2,1)S(1)} %broadcast_in_dim.11.refs_2_, ...), custom_call_target="tpu_custom_call" | custom-call | flops 1174405120 | bytes 7864320 | tf_op jit(solution)/shard_map/decode_tiles/pallas_call | solution.py:223
  26.3 0.9 %collective-permute-done.7.refs_8_ = bf16[1024,256]{1,0:T(8,128)(2,1)S(1)} collective-permute-done((bf16[1024,256]{1,0:T(8,128)(2,1)S(1)}, bf16[1024,256]{1,0:T(8,128)(2,1)S(1)}, u32[]{:S(2)}, u32[]{:S(2)}) %collective-permute-start.7) | collective-permute-done | bytes 524320 | tf_op jit(solution)/shard_map/ppermute | solution.py:250
  27.2 0.0 collective-permute-start.11
  27.2 0.5 collective-permute-start.12
  27.7 2.1 %collective-permute-start.8 = (bf16[1024,256]{1,0:T(8,128)(2,1)S(1)}, bf16[1024,256]{1,0:T(8,128)(2,1)S(1)}, u32[]{:S(2)}, u32[]{:S(2)}) collective-permute-start(bf16[1024,256]{1,0:T(8,128)(2,1)S(1)} %collective-permute-done.7.refs_8_), channel_id=1, source_target_pairs={{0,4},{1,3},{4,8},{5,1},{8,12},{9,5},{12,14},{13,9},{14,10},{15,13... | collective-permute-start | bytes 1572872 | tf_op jit(solution)/shard_map/ppermute | solution.py:250
  29.8 3.0 %collective-permute-done.2.refs_7_ = bf16[1024,256]{1,0:T(8,128)(2,1)S(1)} collective-permute-done((bf16[1024,256]{1,0:T(8,128)(2,1)S(1)}, bf16[1024,256]{1,0:T(8,128)(2,1)S(1)}, u32[]{:S(2)}, u32[]{:S(2)}) %collective-permute-start.2) | collective-permute-done | bytes 524320 | tf_op jit(solution)/shard_map/ppermute | solution.py:250
  32.8 2.1 %collective-permute-start.3 = (bf16[1024,256]{1,0:T(8,128)(2,1)S(1)}, bf16[1024,256]{1,0:T(8,128)(2,1)S(1)}, u32[]{:S(2)}, u32[]{:S(2)}) collective-permute-start(bf16[1024,256]{1,0:T(8,128)(2,1)S(1)} %collective-permute-done.2.refs_7_), channel_id=1, source_target_pairs={{0,4},{1,3},{4,8},{5,1},{8,12},{9,5},{12,14},{13,9},{14,10},{15,13... | collective-permute-start | bytes 1572872 | tf_op jit(solution)/shard_map/ppermute | solution.py:250
  34.9 0.0 collective-permute-done.11.refs_9_
  34.9 0.0 collective-permute-done.12.refs_10_
  34.9 2.5 %decode_tiles.5 = (bf16[48,4096]{1,0:T(8,128)(2,1)S(1)}, bf16[48,4096]{1,0:T(8,128)(2,1)S(1)}, bf16[32,128,512]{2,1,0:T(8,128)(2,1)S(1)}) custom-call(s32[424]{0:T(512)S(1)} %get-tuple-element.47.refs_0_, bf16[512,512]{1,0:T(8,128)(2,1)S(1)} %get-tuple-element.48.refs_1_, ...), custom_call_target="tpu_custom_call", output_to_operand_aliasing={{0}: (11, {}), {1}: (12, {}), {2}: (13, {})} | custom-call | flops 1174405120 | bytes 7864320 | tf_op jit(solution)/shard_map/decode_tiles/pallas_call | solution.py:223
  37.4 1.0 %collective-permute-done.8.refs_8_ = bf16[1024,256]{1,0:T(8,128)(2,1)S(1)} collective-permute-done((bf16[1024,256]{1,0:T(8,128)(2,1)S(1)}, bf16[1024,256]{1,0:T(8,128)(2,1)S(1)}, u32[]{:S(2)}, u32[]{:S(2)}) %collective-permute-start.8) | collective-permute-done | bytes 524320 | tf_op jit(solution)/shard_map/ppermute | solution.py:250
  38.4 0.0 collective-permute-start.13
  38.4 0.5 collective-permute-start.14
  38.9 5.1 %collective-permute-done.3.refs_7_ = bf16[1024,256]{1,0:T(8,128)(2,1)S(1)} collective-permute-done((bf16[1024,256]{1,0:T(8,128)(2,1)S(1)}, bf16[1024,256]{1,0:T(8,128)(2,1)S(1)}, u32[]{:S(2)}, u32[]{:S(2)}) %collective-permute-start.3) | collective-permute-done | bytes 524320 | tf_op jit(solution)/shard_map/ppermute | solution.py:250
  44.0 0.0 collective-permute-start.4
  44.0 0.0 collective-permute-done.13.refs_9_
  44.1 0.0 collective-permute-done.14.refs_10_
  44.1 1.9 %decode_tiles.6 = (bf16[48,4096]{1,0:T(8,128)(2,1)S(1)}, bf16[48,4096]{1,0:T(8,128)(2,1)S(1)}, bf16[32,128,512]{2,1,0:T(8,128)(2,1)S(1)}) custom-call(s32[424]{0:T(512)S(1)} %get-tuple-element.47.refs_0_, bf16[512,512]{1,0:T(8,128)(2,1)S(1)} %get-tuple-element.48.refs_1_, ...), custom_call_target="tpu_custom_call", output_to_operand_aliasing={{0}: (11, {}), {1}: (12, {}), {2}: (13, {})} | custom-call | flops 1174405120 | bytes 7864320 | tf_op jit(solution)/shard_map/decode_tiles/pallas_call | solution.py:223
  45.9 0.0 collective-permute-done.4.refs_8_
  46.0 4.2 %decode_tiles.7 = (bf16[48,4096]{1,0:T(8,128)(2,1)S(1)}, bf16[48,4096]{1,0:T(8,128)(2,1)S(1)}, bf16[32,128,512]{2,1,0:T(8,128)(2,1)S(1)}) custom-call(s32[424]{0:T(512)S(1)} %get-tuple-element.47.refs_0_, bf16[512,512]{1,0:T(8,128)(2,1)S(1)} %get-tuple-element.48.refs_1_, ...), custom_call_target="tpu_custom_call", output_to_operand_aliasing={{0}: (9, {}), {1}: (10, {}), {2}: (11, {})} | custom-call | flops 1174405120 | bytes 7864320 | tf_op jit(solution)/shard_map/decode_tiles/pallas_call | solution.py:223
  50.2 2.3 %collective-permute-start.15 = (bf16[48,4096]{1,0:T(8,128)(2,1)S(1)}, bf16[48,4096]{1,0:T(8,128)(2,1)S(1)}, u32[]{:S(2)}, u32[]{:S(2)}) collective-permute-start(bf16[48,4096]{1,0:T(8,128)(2,1)S(1)} %get-tuple-element.76), channel_id=1, source_target_pairs={{0,1},{1,0},{2,3},{3,2},{4,5},{5,4},{6,7},{7,6},{8,9},{9,8},{10,11... | collective-permute-start | bytes 1179656 | tf_op jit(solution)/shard_map/ppermute | solution.py:253
  52.4 1.3 %collective-permute-done.15 = bf16[48,4096]{1,0:T(8,128)(2,1)S(1)} collective-permute-done((bf16[48,4096]{1,0:T(8,128)(2,1)S(1)}, bf16[48,4096]{1,0:T(8,128)(2,1)S(1)}, u32[]{:S(2)}, u32[]{:S(2)}) %collective-permute-start.15) | collective-permute-done | bytes 393248 | tf_op jit(solution)/shard_map/ppermute | solution.py:253
  53.9 0.9 %pad_maximum_fusion = bf16[40,8192]{1,0:T(8,128)(2,1)} fusion(bf16[40,4096]{1,0:T(8,128)(2,1)S(1)} %get-tuple-element.78, bf16[40,4096]{1,0:T(8,128)(2,1)S(1)} %get-tuple-element.77), kind=kLoop, calls=%fused_computation | loop fusion | flops 1310720 | bytes 1310720 | tf_op jit(solution)/shard_map/concatenate | solution.py:331
  (1 shorter events, 0.0 us)
Async XLA Ops:
  0.0 3.0 %collective-permute-start.5 = (bf16[1024,256]{1,0:T(8,128)(2,1)}, bf16[1024,256]{1,0:T(8,128)(2,1)S(1)}, u32[]{:S(2)}, u32[]{:S(2)}) collective-permute-start(bf16[1024,256]{1,0:T(8,128)(2,1)} %refs_8_.1), channel_id=1, source_target_pairs={{0,1},{1,0},{2,3},{3,2},{4,5},{5,4},{6,7},{7,6},{8,9},{9,8},{10,11... | collective-permute-start | bytes 1572872 | tf_op jit(solution)/shard_map/ppermute | solution.py:253
  0.5 9.9 %collective-permute-start = (bf16[1024,256]{1,0:T(8,128)(2,1)}, bf16[1024,256]{1,0:T(8,128)(2,1)S(1)}, u32[]{:S(2)}, u32[]{:S(2)}) collective-permute-start(bf16[1024,256]{1,0:T(8,128)(2,1)} %refs_8_.1), channel_id=1, source_target_pairs={{0,4},{1,3},{4,8},{5,1},{8,12},{9,5},{12,14},{13,9},{14,10},{15,13... | collective-permute-start | bytes 1572872 | tf_op jit(solution)/shard_map/ppermute | solution.py:250
  3.0 12.9 %collective-permute-start.6 = (bf16[1024,256]{1,0:T(8,128)(2,1)S(1)}, bf16[1024,256]{1,0:T(8,128)(2,1)S(1)}, u32[]{:S(2)}, u32[]{:S(2)}) collective-permute-start(bf16[1024,256]{1,0:T(8,128)(2,1)S(1)} %collective-permute-done.5.refs_8_), channel_id=1, source_target_pairs={{0,4},{1,3},{4,8},{5,1},{8,12},{9,5},{12,14},{13,9},{14,10},{15,13... | collective-permute-start | bytes 1572872 | tf_op jit(solution)/shard_map/ppermute | solution.py:250
  10.4 11.2 %collective-permute-start.1 = (bf16[1024,256]{1,0:T(8,128)(2,1)S(1)}, bf16[1024,256]{1,0:T(8,128)(2,1)S(1)}, u32[]{:S(2)}, u32[]{:S(2)}) collective-permute-start(bf16[1024,256]{1,0:T(8,128)(2,1)S(1)} %collective-permute-done.refs_9_), channel_id=1, source_target_pairs={{0,4},{1,3},{4,8},{5,1},{8,12},{9,5},{12,14},{13,9},{14,10},{15,13... | collective-permute-start | bytes 1572872 | tf_op jit(solution)/shard_map/ppermute | solution.py:250
  12.4 11.2 %collective-permute-start.10 = (bf16[1024,256]{1,0:T(8,128)(2,1)S(1)}, bf16[1024,256]{1,0:T(8,128)(2,1)S(1)}, u32[]{:S(2)}, u32[]{:S(2)}) collective-permute-start(bf16[1024,256]{1,0:T(8,128)(2,1)S(1)} %collective-permute-done.refs_9_), channel_id=1, source_target_pairs={{0,1},{1,0},{2,3},{3,2},{4,5},{5,4},{6,7},{7,6},{8,9},{9,8},{10,11... | collective-permute-start | bytes 1572872 | tf_op jit(solution)/shard_map/ppermute | solution.py:253
  16.0 7.7 %collective-permute-start.9 = (bf16[1024,256]{1,0:T(8,128)(2,1)S(1)}, bf16[1024,256]{1,0:T(8,128)(2,1)S(1)}, u32[]{:S(2)}, u32[]{:S(2)}) collective-permute-start(bf16[1024,256]{1,0:T(8,128)(2,1)S(1)} %collective-permute-done.6.refs_10_), channel_id=1, source_target_pairs={{0,1},{1,0},{2,3},{3,2},{4,5},{5,4},{6,7},{7,6},{8,9},{9,8},{10,11... | collective-permute-start | bytes 1572872 | tf_op jit(solution)/shard_map/ppermute | solution.py:253
  16.0 11.2 %collective-permute-start.7 = (bf16[1024,256]{1,0:T(8,128)(2,1)S(1)}, bf16[1024,256]{1,0:T(8,128)(2,1)S(1)}, u32[]{:S(2)}, u32[]{:S(2)}) collective-permute-start(bf16[1024,256]{1,0:T(8,128)(2,1)S(1)} %collective-permute-done.6.refs_10_), channel_id=1, source_target_pairs={{0,4},{1,3},{4,8},{5,1},{8,12},{9,5},{12,14},{13,9},{14,10},{15,13... | collective-permute-start | bytes 1572872 | tf_op jit(solution)/shard_map/ppermute | solution.py:250
  21.6 11.2 %collective-permute-start.2 = (bf16[1024,256]{1,0:T(8,128)(2,1)S(1)}, bf16[1024,256]{1,0:T(8,128)(2,1)S(1)}, u32[]{:S(2)}, u32[]{:S(2)}) collective-permute-start(bf16[1024,256]{1,0:T(8,128)(2,1)S(1)} %collective-permute-done.1.refs_7_), channel_id=1, source_target_pairs={{0,4},{1,3},{4,8},{5,1},{8,12},{9,5},{12,14},{13,9},{14,10},{15,13... | collective-permute-start | bytes 1572872 | tf_op jit(solution)/shard_map/ppermute | solution.py:250
  27.2 7.7 %collective-permute-start.11 = (bf16[1024,256]{1,0:T(8,128)(2,1)S(1)}, bf16[1024,256]{1,0:T(8,128)(2,1)S(1)}, u32[]{:S(2)}, u32[]{:S(2)}) collective-permute-start(bf16[1024,256]{1,0:T(8,128)(2,1)S(1)} %collective-permute-done.7.refs_8_), channel_id=1, source_target_pairs={{0,1},{1,0},{2,3},{3,2},{4,5},{5,4},{6,7},{7,6},{8,9},{9,8},{10,11... | collective-permute-start | bytes 1572872 | tf_op jit(solution)/shard_map/ppermute | solution.py:253
  27.2 7.7 %collective-permute-start.12 = (bf16[1024,256]{1,0:T(8,128)(2,1)S(1)}, bf16[1024,256]{1,0:T(8,128)(2,1)S(1)}, u32[]{:S(2)}, u32[]{:S(2)}) collective-permute-start(bf16[1024,256]{1,0:T(8,128)(2,1)S(1)} %collective-permute-done.1.refs_7_), channel_id=1, source_target_pairs={{0,1},{1,0},{2,3},{3,2},{4,5},{5,4},{6,7},{7,6},{8,9},{9,8},{10,11... | collective-permute-start | bytes 1572872 | tf_op jit(solution)/shard_map/ppermute | solution.py:253
  27.7 10.7 %collective-permute-start.8 = (bf16[1024,256]{1,0:T(8,128)(2,1)S(1)}, bf16[1024,256]{1,0:T(8,128)(2,1)S(1)}, u32[]{:S(2)}, u32[]{:S(2)}) collective-permute-start(bf16[1024,256]{1,0:T(8,128)(2,1)S(1)} %collective-permute-done.7.refs_8_), channel_id=1, source_target_pairs={{0,4},{1,3},{4,8},{5,1},{8,12},{9,5},{12,14},{13,9},{14,10},{15,13... | collective-permute-start | bytes 1572872 | tf_op jit(solution)/shard_map/ppermute | solution.py:250
  32.8 11.2 %collective-permute-start.3 = (bf16[1024,256]{1,0:T(8,128)(2,1)S(1)}, bf16[1024,256]{1,0:T(8,128)(2,1)S(1)}, u32[]{:S(2)}, u32[]{:S(2)}) collective-permute-start(bf16[1024,256]{1,0:T(8,128)(2,1)S(1)} %collective-permute-done.2.refs_7_), channel_id=1, source_target_pairs={{0,4},{1,3},{4,8},{5,1},{8,12},{9,5},{12,14},{13,9},{14,10},{15,13... | collective-permute-start | bytes 1572872 | tf_op jit(solution)/shard_map/ppermute | solution.py:250
  38.4 5.6 %collective-permute-start.13 = (bf16[1024,256]{1,0:T(8,128)(2,1)S(1)}, bf16[1024,256]{1,0:T(8,128)(2,1)S(1)}, u32[]{:S(2)}, u32[]{:S(2)}) collective-permute-start(bf16[1024,256]{1,0:T(8,128)(2,1)S(1)} %collective-permute-done.8.refs_8_), channel_id=1, source_target_pairs={{0,1},{1,0},{2,3},{3,2},{4,5},{5,4},{6,7},{7,6},{8,9},{9,8},{10,11... | collective-permute-start | bytes 1572872 | tf_op jit(solution)/shard_map/ppermute | solution.py:253
  38.4 5.6 %collective-permute-start.14 = (bf16[1024,256]{1,0:T(8,128)(2,1)S(1)}, bf16[1024,256]{1,0:T(8,128)(2,1)S(1)}, u32[]{:S(2)}, u32[]{:S(2)}) collective-permute-start(bf16[1024,256]{1,0:T(8,128)(2,1)S(1)} %collective-permute-done.2.refs_7_), channel_id=1, source_target_pairs={{0,1},{1,0},{2,3},{3,2},{4,5},{5,4},{6,7},{7,6},{8,9},{9,8},{10,11... | collective-permute-start | bytes 1572872 | tf_op jit(solution)/shard_map/ppermute | solution.py:253
  44.0 1.9 %collective-permute-start.4 = (bf16[1024,256]{1,0:T(8,128)(2,1)S(1)}, bf16[1024,256]{1,0:T(8,128)(2,1)S(1)}, u32[]{:S(2)}, u32[]{:S(2)}) collective-permute-start(bf16[1024,256]{1,0:T(8,128)(2,1)S(1)} %collective-permute-done.3.refs_7_), channel_id=1, source_target_pairs={{0,1},{1,0},{2,3},{3,2},{4,5},{5,4},{6,7},{7,6},{8,9},{9,8},{10,11... | collective-permute-start | bytes 1572872 | tf_op jit(solution)/shard_map/ppermute | solution.py:253
  50.2 3.6 %collective-permute-start.15 = (bf16[48,4096]{1,0:T(8,128)(2,1)S(1)}, bf16[48,4096]{1,0:T(8,128)(2,1)S(1)}, u32[]{:S(2)}, u32[]{:S(2)}) collective-permute-start(bf16[48,4096]{1,0:T(8,128)(2,1)S(1)} %get-tuple-element.76), channel_id=1, source_target_pairs={{0,1},{1,0},{2,3},{3,2},{4,5},{5,4},{6,7},{7,6},{8,9},{9,8},{10,11... | collective-permute-start | bytes 1179656 | tf_op jit(solution)/shard_map/ppermute | solution.py:253

commit v3 on v2

--- a/solution.py
+++ b/solution.py
@@ -40,8 +40,8 @@
     first_stage = stages_of(count)[0]
 
     listed = wanted.shape[1]
-    entry_work = tiles * META + len(stages_of(count)) * (tiles + 1)
-    for stage in range(len(stages_of(count))):
+    entry_work = tiles * META + len(levels_of(count)) * (tiles + 1)
+    for stage in range(len(levels_of(count))):
         meta[tiles * META + stage * (tiles + 1)] = 0
         meta[entry_work + stage * (listed + 1)] = 0
 
@@ -50,7 +50,12 @@
         behind = here - place(lax.div(block, blocks))
         behind = jnp.where(core == 0, behind, -behind)
         behind = jnp.where(behind < 0, behind + count, behind)
-        stage = jnp.maximum(jnp.minimum(behind, count - behind), first_stage) - first_stage
+        distance = jnp.minimum(behind, count - behind)
+        stage = jnp.maximum(distance, first_stage) - first_stage
+        far = count // 2
+        if first_stage < far - 1:
+            second = jnp.logical_or(distance == far, jnp.logical_and(distance == far - 1, behind > far))
+            stage = stage + second.astype(jnp.int32)
         entry_stage[entry] = stage
         work = entry_work + stage * (listed + 1)
         meta[work] = meta[work] + 1
@@ -109,7 +114,7 @@
     return pl.pallas_call(
         lambda *refs: prepare_kernel(count, columns, blocks, *refs),
         out_shape=[
-            jax.ShapeDtypeStruct((tiles * META + len(stages_of(count)) * (tiles + wanted.shape[1] + 2),), jnp.int32),
+            jax.ShapeDtypeStruct((tiles * META + len(levels_of(count)) * (tiles + wanted.shape[1] + 2),), jnp.int32),
             jax.ShapeDtypeStruct((rows, w_out.shape[1]), jnp.bfloat16),
             jax.ShapeDtypeStruct((rows, 1), jnp.float32),
             jax.ShapeDtypeStruct((rows, state.shape[1]), jnp.bfloat16),
@@ -129,6 +134,18 @@
 def stages_of(count):
     far = count // 2
     return list(range(max(far - 3, 1), far + 1))
+
+
+def levels_of(count):
+    far, levels = count // 2, []
+    for d in stages_of(count):
+        if d == stages_of(count)[0]:
+            levels.append([p for p in range(count) if min(p, count - p) <= d])
+        elif d == far - 1:
+            levels += [[d], [count - d]]
+        else:
+            levels.append(sorted({d, count - d}))
+    return levels
 
 
 def decode_kernel(stage, stages, blocks, pieces, tiles, held, *refs):
@@ -270,7 +287,7 @@
         core = lax.axis_index("writer")
         tiles = interp.shape[0] // 2
         each = w_out.shape[1] // 2
-        stages = stages_of(count)
+        stages, levels = stages_of(count), levels_of(count)
         meta, heads, bias, state, w_in, nodes_kept, interp_kept = prepare(
             count,
             columns,
@@ -292,13 +309,12 @@
         other_nodes = swap(mesh_nodes)
         same, cross = [mesh_nodes], [other_nodes]
         table = {0: (nodes_kept, other_nodes)}
-        def decode(d, outs):
-            distances = range(d + 1) if d == stages[0] else (d,)
-            pieces = [p for p in sorted(table) if min(p, count - p) in distances]
+        def decode(level, outs):
+            pieces = levels[level]
             return list(
                 decode_tiles(
-                    stages.index(d),
-                    len(stages),
+                    level,
+                    len(levels),
                     blocks,
                     pieces,
                     tiles,
@@ -309,23 +325,28 @@
                 )
             )
 
-        for d in range(1, far + 1):
+        level = 0
+        for d in range(1, far):
             if d == 2:
                 same[-1], small = lax.optimization_barrier((same[-1], small))
             same.append(send_on(same[-1]))
-            if d < far:
-                cross.append(send_on(cross[-1]))
-            swapped = (cross[-1], same[-1])
+            cross.append(send_on(cross[-1]))
+            table[d] = (same[d], cross[d])
+            swapped = (cross[d], same[d])
             if d - 1 in stages:
-                outs = decode(d - 1, outs)
-                if d < far:
+                outs, level = decode(level, outs), level + 1
+                if d == far - 1:
+                    last, outs = lax.optimization_barrier((same[d], outs))
+                    outs, level = decode(level, outs), level + 1
+                    first, outs = lax.optimization_barrier((cross[d], outs))
+                    swapped = (first, last)
+                else:
                     *swapped, outs = lax.optimization_barrier((*swapped, outs))
-            if d < far:
-                table[d] = (same[d], cross[d])
-                table[count - d] = (swap(swapped[0]), swap(swapped[1]))
-            else:
-                table[d] = (same[d], swap(swapped[1]))
-        outs = decode(far, outs)
+            table[count - d] = (swap(swapped[0]), swap(swapped[1]))
+        same.append(send_on(same[-1]))
+        outs = decode(level, outs)
+        table[far] = (same[far], swap(same[far]))
+        outs = decode(level + 1, outs)
         received = swap(outs[1])
         own, received = outs[0][:each], received[:each]
         return jnp.concatenate(

time: 55.2 us -> 54.3 us (0.984)
  starting transfers between devices: 18.8 us -> 17 us
  Pallas kernels: 15.8 us -> 17.4 us
  waiting for transfers between devices: 18.5 us -> 17.3 us
    ppermute x9, starting transfers between devices: 3.77 us -> 2.08 us  [swap(): return lax.ppermute(piece, 'writer', [(0, 1), (1, 0)])]
    pallas_call x4 -> x5, Pallas kernels: 11.2 us -> 12.8 us  [decode_tiles(): pl.pallas_call(lambda *refs: decode_kernel(stage, stages, blocks, pieces,...]
    ppermute x7, waiting for transfers between devices: 17.1 us -> 16 us  [send_on(): return lax.ppermute(piece, ('mesh', 'writer'), onward)]
  transfers between devices with their start and end apart: 16 -> 16, of which waited for: 7 -> 7; matrix products, arithmetic and copies ran while one was open for 1% -> 1% of each run, Pallas kernels for 21% -> 25%
where the time goes in v3:
time: 54.3 us; the launch traced here: 53.5 us
  Pallas kernels  17.4 us (32%)
  waiting for transfers between devices  17.3 us (32%)
  starting transfers between devices  17 us (31%)
  other arithmetic  0.93 us (2%)
  local copies, waits for them, and re-layouts  0.68 us (1%)
    ppermute x7, waiting for transfers between devices, send_on(): return lax.ppermute(piece, ('mesh', 'writer'), onward)  16 us
    ppermute x7, starting transfers between devices, send_on(): return lax.ppermute(piece, ('mesh', 'writer'), onward)  15 us
    pallas_call x5, Pallas kernels, decode_tiles(): pl.pallas_call(lambda *refs: decode_kernel(stage, stages, blocks, pieces,...  12.8 us
    pallas_call x1, Pallas kernels, prepare(): pl.pallas_call(lambda *refs: prepare_kernel(count, columns, blocks, *refs...  4.63 us
    ppermute x9, starting transfers between devices, swap(): return lax.ppermute(piece, 'writer', [(0, 1), (1, 0)])  2.08 us
    ppermute x9, waiting for transfers between devices, swap(): return lax.ppermute(piece, 'writer', [(0, 1), (1, 0)])  1.37 us
  transfers between devices with their start and end apart: 16, of which 7 were waited for; matrix products, arithmetic and copies ran while one was open for 1% of the time, Pallas kernels for 25%

profile of v3, /device:TPU:0, one launch (start us, length us, event | category | flops | bytes accessed | tf_op | source)
XLA Modules:
  0.0 53.5 jit_solution(13327201688510770196)
XLA Ops:
  0.0 0.5 collective-permute-start.5
  0.5 2.6 %collective-permute-start = (bf16[1024,256]{1,0:T(8,128)(2,1)}, bf16[1024,256]{1,0:T(8,128)(2,1)S(1)}, u32[]{:S(2)}, u32[]{:S(2)}) collective-permute-start(bf16[1024,256]{1,0:T(8,128)(2,1)} %refs_8_.1), channel_id=1, source_target_pairs={{0,4},{1,3},{4,8},{5,1},{8,12},{9,5},{12,14},{13,9},{14,10},{15,13... | collective-permute-start | bytes 1572872 | tf_op jit(solution)/shard_map/ppermute | solution.py:267
  3.0 0.0 collective-permute-done.5.refs_8_
  3.0 2.1 %collective-permute-start.6 = (bf16[1024,256]{1,0:T(8,128)(2,1)S(1)}, bf16[1024,256]{1,0:T(8,128)(2,1)S(1)}, u32[]{:S(2)}, u32[]{:S(2)}) collective-permute-start(bf16[1024,256]{1,0:T(8,128)(2,1)S(1)} %collective-permute-done.5.refs_8_), channel_id=1, source_target_pairs={{0,4},{1,3},{4,8},{5,1},{8,12},{9,5},{12,14},{13,9},{14,10},{15,13... | collective-permute-start | bytes 1572872 | tf_op jit(solution)/shard_map/ppermute | solution.py:267
  5.1 0.7 %broadcast_in_dim.11.refs_2_ = bf16[1,512]{1,0:T(2,128)(2,1)S(1)} reshape(bf16[512]{0:T(512)(128)(2,1)} %param.18) | data formatting | bytes 2048 | tf_op jit(solution)/shard_map/broadcast_in_dim | solution.py:306
  5.8 4.6 %prepare.1 = (s32[490]{0:T(512)S(1)}, bf16[96,512]{1,0:T(8,128)(2,1)S(1)}, f32[96,1]{1,0:T(8,128)S(1)}, bf16[96,4096]{1,0:T(8,128)(2,1)S(1)}, bf16[512,512]{1,0:...) custom-call(s32[1,32]{1,0:T(1,128)} %refs_0_.1, s32[4,64]{1,0:T(4,128)} %bitcast.5, ...), custom_call_target="tpu_custom_call" | custom-call | flops 62914560 | bytes 1966080 | tf_op jit(solution)/shard_map/prepare/pallas_call | solution.py:114
  10.5 0.0 collective-permute-done.refs_9_
  10.5 1.9 %collective-permute-start.1 = (bf16[1024,256]{1,0:T(8,128)(2,1)S(1)}, bf16[1024,256]{1,0:T(8,128)(2,1)S(1)}, u32[]{:S(2)}, u32[]{:S(2)}) collective-permute-start(bf16[1024,256]{1,0:T(8,128)(2,1)S(1)} %collective-permute-done.refs_9_), channel_id=1, source_target_pairs={{0,4},{1,3},{4,8},{5,1},{8,12},{9,5},{12,14},{13,9},{14,10},{15,13... | collective-permute-start | bytes 1572872 | tf_op jit(solution)/shard_map/ppermute | solution.py:267
  12.4 0.0 collective-permute-start.10
  12.4 3.5 %collective-permute-done.6.refs_10_ = bf16[1024,256]{1,0:T(8,128)(2,1)S(1)} collective-permute-done((bf16[1024,256]{1,0:T(8,128)(2,1)S(1)}, bf16[1024,256]{1,0:T(8,128)(2,1)S(1)}, u32[]{:S(2)}, u32[]{:S(2)}) %collective-permute-start.6) | collective-permute-done | bytes 524320 | tf_op jit(solution)/shard_map/ppermute | solution.py:267
  16.0 0.0 collective-permute-start.9
  16.0 2.1 %collective-permute-start.7 = (bf16[1024,256]{1,0:T(8,128)(2,1)S(1)}, bf16[1024,256]{1,0:T(8,128)(2,1)S(1)}, u32[]{:S(2)}, u32[]{:S(2)}) collective-permute-start(bf16[1024,256]{1,0:T(8,128)(2,1)S(1)} %collective-permute-done.6.refs_10_), channel_id=1, source_target_pairs={{0,4},{1,3},{4,8},{5,1},{8,12},{9,5},{12,14},{13,9},{14,10},{15,13... | collective-permute-start | bytes 1572872 | tf_op jit(solution)/shard_map/ppermute | solution.py:267
  18.0 3.5 %collective-permute-done.1.refs_7_ = bf16[1024,256]{1,0:T(8,128)(2,1)S(1)} collective-permute-done((bf16[1024,256]{1,0:T(8,128)(2,1)S(1)}, bf16[1024,256]{1,0:T(8,128)(2,1)S(1)}, u32[]{:S(2)}, u32[]{:S(2)}) %collective-permute-start.1) | collective-permute-done | bytes 524320 | tf_op jit(solution)/shard_map/ppermute | solution.py:267
  21.6 2.1 %collective-permute-start.2 = (bf16[1024,256]{1,0:T(8,128)(2,1)S(1)}, bf16[1024,256]{1,0:T(8,128)(2,1)S(1)}, u32[]{:S(2)}, u32[]{:S(2)}) collective-permute-start(bf16[1024,256]{1,0:T(8,128)(2,1)S(1)} %collective-permute-done.1.refs_7_), channel_id=1, source_target_pairs={{0,4},{1,3},{4,8},{5,1},{8,12},{9,5},{12,14},{13,9},{14,10},{15,13... | collective-permute-start | bytes 1572872 | tf_op jit(solution)/shard_map/ppermute | solution.py:267
  23.7 0.0 collective-permute-done.10.refs_12_
  23.7 0.0 collective-permute-done.9.refs_11_
  23.7 2.7 %decode_tiles.5 = (bf16[48,4096]{1,0:T(8,128)(2,1)S(1)}, bf16[48,4096]{1,0:T(8,128)(2,1)S(1)}, bf16[32,128,512]{2,1,0:T(8,128)(2,1)S(1)}) custom-call(s32[490]{0:T(512)S(1)} %get-tuple-element.53.refs_0_, bf16[512,512]{1,0:T(8,128)(2,1)S(1)} %get-tuple-element.54.refs_1_, bf16[1,512]{1,0:T(2,128)(2,1)S(1)} %broadcast_in_dim.11.refs_2_, ...), custom_call_target="tpu_custom_call" | custom-call | flops 1174405120 | bytes 7864320 | tf_op jit(solution)/shard_map/decode_tiles/pallas_call | solution.py:240
  26.3 0.9 %collective-permute-done.7.refs_8_ = bf16[1024,256]{1,0:T(8,128)(2,1)S(1)} collective-permute-done((bf16[1024,256]{1,0:T(8,128)(2,1)S(1)}, bf16[1024,256]{1,0:T(8,128)(2,1)S(1)}, u32[]{:S(2)}, u32[]{:S(2)}) %collective-permute-start.7) | collective-permute-done | bytes 524320 | tf_op jit(solution)/shard_map/ppermute | solution.py:267
  27.2 0.0 collective-permute-start.11
  27.2 0.5 collective-permute-start.12
  27.7 2.1 %collective-permute-start.8 = (bf16[1024,256]{1,0:T(8,128)(2,1)S(1)}, bf16[1024,256]{1,0:T(8,128)(2,1)S(1)}, u32[]{:S(2)}, u32[]{:S(2)}) collective-permute-start(bf16[1024,256]{1,0:T(8,128)(2,1)S(1)} %collective-permute-done.7.refs_8_), channel_id=1, source_target_pairs={{0,4},{1,3},{4,8},{5,1},{8,12},{9,5},{12,14},{13,9},{14,10},{15,13... | collective-permute-start | bytes 1572872 | tf_op jit(solution)/shard_map/ppermute | solution.py:267
  29.8 3.0 %collective-permute-done.2.refs_7_ = bf16[1024,256]{1,0:T(8,128)(2,1)S(1)} collective-permute-done((bf16[1024,256]{1,0:T(8,128)(2,1)S(1)}, bf16[1024,256]{1,0:T(8,128)(2,1)S(1)}, u32[]{:S(2)}, u32[]{:S(2)}) %collective-permute-start.2) | collective-permute-done | bytes 524320 | tf_op jit(solution)/shard_map/ppermute | solution.py:267
  32.8 2.1 %collective-permute-start.3 = (bf16[1024,256]{1,0:T(8,128)(2,1)S(1)}, bf16[1024,256]{1,0:T(8,128)(2,1)S(1)}, u32[]{:S(2)}, u32[]{:S(2)}) collective-permute-start(bf16[1024,256]{1,0:T(8,128)(2,1)S(1)} %collective-permute-done.2.refs_7_), channel_id=1, source_target_pairs={{0,4},{1,3},{4,8},{5,1},{8,12},{9,5},{12,14},{13,9},{14,10},{15,13... | collective-permute-start | bytes 1572872 | tf_op jit(solution)/shard_map/ppermute | solution.py:267
  34.9 0.0 collective-permute-done.11.refs_9_
  34.9 0.0 collective-permute-done.12.refs_10_
  34.9 1.9 %decode_tiles.6 = (bf16[48,4096]{1,0:T(8,128)(2,1)S(1)}, bf16[48,4096]{1,0:T(8,128)(2,1)S(1)}, bf16[32,128,512]{2,1,0:T(8,128)(2,1)S(1)}) custom-call(s32[490]{0:T(512)S(1)} %get-tuple-element.53.refs_0_, bf16[512,512]{1,0:T(8,128)(2,1)S(1)} %get-tuple-element.54.refs_1_, ...), custom_call_target="tpu_custom_call", output_to_operand_aliasing={{0}: (11, {}), {1}: (12, {}), {2}: (13, {})} | custom-call | flops 1174405120 | bytes 7864320 | tf_op jit(solution)/shard_map/decode_tiles/pallas_call | solution.py:240
  36.8 1.7 %collective-permute-done.8.refs_8_ = bf16[1024,256]{1,0:T(8,128)(2,1)S(1)} collective-permute-done((bf16[1024,256]{1,0:T(8,128)(2,1)S(1)}, bf16[1024,256]{1,0:T(8,128)(2,1)S(1)}, u32[]{:S(2)}, u32[]{:S(2)}) %collective-permute-start.8) | collective-permute-done | bytes 524320 | tf_op jit(solution)/shard_map/ppermute | solution.py:267
  38.4 1.7 %decode_tiles.7 = (bf16[48,4096]{1,0:T(8,128)(2,1)S(1)}, bf16[48,4096]{1,0:T(8,128)(2,1)S(1)}, bf16[32,128,512]{2,1,0:T(8,128)(2,1)S(1)}) custom-call(s32[490]{0:T(512)S(1)} %get-tuple-element.53.refs_0_, bf16[512,512]{1,0:T(8,128)(2,1)S(1)} %get-tuple-element.54.refs_1_, ...), custom_call_target="tpu_custom_call", output_to_operand_aliasing={{0}: (9, {}), {1}: (10, {}), {2}: (11, {})} | custom-call | flops 1174405120 | bytes 7864320 | tf_op jit(solution)/shard_map/decode_tiles/pallas_call | solution.py:240
  40.1 0.1 collective-permute-start.13
  40.2 0.5 collective-permute-start.14
  40.7 3.3 %collective-permute-done.3.refs_7_ = bf16[1024,256]{1,0:T(8,128)(2,1)S(1)} collective-permute-done((bf16[1024,256]{1,0:T(8,128)(2,1)S(1)}, bf16[1024,256]{1,0:T(8,128)(2,1)S(1)}, u32[]{:S(2)}, u32[]{:S(2)}) %collective-permute-start.3) | collective-permute-done | bytes 524320 | tf_op jit(solution)/shard_map/ppermute | solution.py:267
  44.0 0.0 collective-permute-start.4
  44.0 0.0 collective-permute-done.13.refs_7_
  44.1 0.0 collective-permute-done.14.refs_8_
  44.1 2.4 %decode_tiles.8 = (bf16[48,4096]{1,0:T(8,128)(2,1)S(1)}, bf16[48,4096]{1,0:T(8,128)(2,1)S(1)}, bf16[32,128,512]{2,1,0:T(8,128)(2,1)S(1)}) custom-call(s32[490]{0:T(512)S(1)} %get-tuple-element.53.refs_0_, bf16[512,512]{1,0:T(8,128)(2,1)S(1)} %get-tuple-element.54.refs_1_, ...), custom_call_target="tpu_custom_call", output_to_operand_aliasing={{0}: (9, {}), {1}: (10, {}), {2}: (11, {})} | custom-call | flops 1174405120 | bytes 7864320 | tf_op jit(solution)/shard_map/decode_tiles/pallas_call | solution.py:240
  46.5 0.0 collective-permute-done.4.refs_8_
  46.5 4.2 %decode_tiles.9 = (bf16[48,4096]{1,0:T(8,128)(2,1)S(1)}, bf16[48,4096]{1,0:T(8,128)(2,1)S(1)}, bf16[32,128,512]{2,1,0:T(8,128)(2,1)S(1)}) custom-call(s32[490]{0:T(512)S(1)} %get-tuple-element.53.refs_0_, bf16[512,512]{1,0:T(8,128)(2,1)S(1)} %get-tuple-element.54.refs_1_, ...), custom_call_target="tpu_custom_call", output_to_operand_aliasing={{0}: (9, {}), {1}: (10, {}), {2}: (11, {})} | custom-call | flops 1174405120 | bytes 7864320 | tf_op jit(solution)/shard_map/decode_tiles/pallas_call | solution.py:240
  50.7 0.5 %collective-permute-start.15 = (bf16[48,4096]{1,0:T(8,128)(2,1)S(1)}, bf16[48,4096]{1,0:T(8,128)(2,1)S(1)}, u32[]{:S(2)}, u32[]{:S(2)}) collective-permute-start(bf16[48,4096]{1,0:T(8,128)(2,1)S(1)} %get-tuple-element.88), channel_id=1, source_target_pairs={{0,1},{1,0},{2,3},{3,2},{4,5},{5,4},{6,7},{7,6},{8,9},{9,8},{10,11... | collective-permute-start | bytes 1179656 | tf_op jit(solution)/shard_map/ppermute | solution.py:270
  51.2 1.3 %collective-permute-done.15 = bf16[48,4096]{1,0:T(8,128)(2,1)S(1)} collective-permute-done((bf16[48,4096]{1,0:T(8,128)(2,1)S(1)}, bf16[48,4096]{1,0:T(8,128)(2,1)S(1)}, u32[]{:S(2)}, u32[]{:S(2)}) %collective-permute-start.15) | collective-permute-done | bytes 393248 | tf_op jit(solution)/shard_map/ppermute | solution.py:270
  52.6 0.9 %pad_maximum_fusion = bf16[40,8192]{1,0:T(8,128)(2,1)} fusion(bf16[40,4096]{1,0:T(8,128)(2,1)S(1)} %get-tuple-element.90, bf16[40,4096]{1,0:T(8,128)(2,1)S(1)} %get-tuple-element.89), kind=kLoop, calls=%fused_computation | loop fusion | flops 1310720 | bytes 1310720 | tf_op jit(solution)/shard_map/concatenate | solution.py:352
  (1 shorter events, 0.0 us)
Async XLA Ops:
  0.0 3.0 %collective-permute-start.5 = (bf16[1024,256]{1,0:T(8,128)(2,1)}, bf16[1024,256]{1,0:T(8,128)(2,1)S(1)}, u32[]{:S(2)}, u32[]{:S(2)}) collective-permute-start(bf16[1024,256]{1,0:T(8,128)(2,1)} %refs_8_.1), channel_id=1, source_target_pairs={{0,1},{1,0},{2,3},{3,2},{4,5},{5,4},{6,7},{7,6},{8,9},{9,8},{10,11... | collective-permute-start | bytes 1572872 | tf_op jit(solution)/shard_map/ppermute | solution.py:270
  0.5 10.0 %collective-permute-start = (bf16[1024,256]{1,0:T(8,128)(2,1)}, bf16[1024,256]{1,0:T(8,128)(2,1)S(1)}, u32[]{:S(2)}, u32[]{:S(2)}) collective-permute-start(bf16[1024,256]{1,0:T(8,128)(2,1)} %refs_8_.1), channel_id=1, source_target_pairs={{0,4},{1,3},{4,8},{5,1},{8,12},{9,5},{12,14},{13,9},{14,10},{15,13... | collective-permute-start | bytes 1572872 | tf_op jit(solution)/shard_map/ppermute | solution.py:267
  3.0 12.9 %collective-permute-start.6 = (bf16[1024,256]{1,0:T(8,128)(2,1)S(1)}, bf16[1024,256]{1,0:T(8,128)(2,1)S(1)}, u32[]{:S(2)}, u32[]{:S(2)}) collective-permute-start(bf16[1024,256]{1,0:T(8,128)(2,1)S(1)} %collective-permute-done.5.refs_8_), channel_id=1, source_target_pairs={{0,4},{1,3},{4,8},{5,1},{8,12},{9,5},{12,14},{13,9},{14,10},{15,13... | collective-permute-start | bytes 1572872 | tf_op jit(solution)/shard_map/ppermute | solution.py:267
  10.5 11.1 %collective-permute-start.1 = (bf16[1024,256]{1,0:T(8,128)(2,1)S(1)}, bf16[1024,256]{1,0:T(8,128)(2,1)S(1)}, u32[]{:S(2)}, u32[]{:S(2)}) collective-permute-start(bf16[1024,256]{1,0:T(8,128)(2,1)S(1)} %collective-permute-done.refs_9_), channel_id=1, source_target_pairs={{0,4},{1,3},{4,8},{5,1},{8,12},{9,5},{12,14},{13,9},{14,10},{15,13... | collective-permute-start | bytes 1572872 | tf_op jit(solution)/shard_map/ppermute | solution.py:267
  12.4 11.2 %collective-permute-start.10 = (bf16[1024,256]{1,0:T(8,128)(2,1)S(1)}, bf16[1024,256]{1,0:T(8,128)(2,1)S(1)}, u32[]{:S(2)}, u32[]{:S(2)}) collective-permute-start(bf16[1024,256]{1,0:T(8,128)(2,1)S(1)} %collective-permute-done.refs_9_), channel_id=1, source_target_pairs={{0,1},{1,0},{2,3},{3,2},{4,5},{5,4},{6,7},{7,6},{8,9},{9,8},{10,11... | collective-permute-start | bytes 1572872 | tf_op jit(solution)/shard_map/ppermute | solution.py:270
  16.0 7.7 %collective-permute-start.9 = (bf16[1024,256]{1,0:T(8,128)(2,1)S(1)}, bf16[1024,256]{1,0:T(8,128)(2,1)S(1)}, u32[]{:S(2)}, u32[]{:S(2)}) collective-permute-start(bf16[1024,256]{1,0:T(8,128)(2,1)S(1)} %collective-permute-done.6.refs_10_), channel_id=1, source_target_pairs={{0,1},{1,0},{2,3},{3,2},{4,5},{5,4},{6,7},{7,6},{8,9},{9,8},{10,11... | collective-permute-start | bytes 1572872 | tf_op jit(solution)/shard_map/ppermute | solution.py:270
  16.0 11.2 %collective-permute-start.7 = (bf16[1024,256]{1,0:T(8,128)(2,1)S(1)}, bf16[1024,256]{1,0:T(8,128)(2,1)S(1)}, u32[]{:S(2)}, u32[]{:S(2)}) collective-permute-start(bf16[1024,256]{1,0:T(8,128)(2,1)S(1)} %collective-permute-done.6.refs_10_), channel_id=1, source_target_pairs={{0,4},{1,3},{4,8},{5,1},{8,12},{9,5},{12,14},{13,9},{14,10},{15,13... | collective-permute-start | bytes 1572872 | tf_op jit(solution)/shard_map/ppermute | solution.py:267
  21.6 11.2 %collective-permute-start.2 = (bf16[1024,256]{1,0:T(8,128)(2,1)S(1)}, bf16[1024,256]{1,0:T(8,128)(2,1)S(1)}, u32[]{:S(2)}, u32[]{:S(2)}) collective-permute-start(bf16[1024,256]{1,0:T(8,128)(2,1)S(1)} %collective-permute-done.1.refs_7_), channel_id=1, source_target_pairs={{0,4},{1,3},{4,8},{5,1},{8,12},{9,5},{12,14},{13,9},{14,10},{15,13... | collective-permute-start | bytes 1572872 | tf_op jit(solution)/shard_map/ppermute | solution.py:267
  27.2 7.7 %collective-permute-start.11 = (bf16[1024,256]{1,0:T(8,128)(2,1)S(1)}, bf16[1024,256]{1,0:T(8,128)(2,1)S(1)}, u32[]{:S(2)}, u32[]{:S(2)}) collective-permute-start(bf16[1024,256]{1,0:T(8,128)(2,1)S(1)} %collective-permute-done.7.refs_8_), channel_id=1, source_target_pairs={{0,1},{1,0},{2,3},{3,2},{4,5},{5,4},{6,7},{7,6},{8,9},{9,8},{10,11... | collective-permute-start | bytes 1572872 | tf_op jit(solution)/shard_map/ppermute | solution.py:270
  27.2 7.7 %collective-permute-start.12 = (bf16[1024,256]{1,0:T(8,128)(2,1)S(1)}, bf16[1024,256]{1,0:T(8,128)(2,1)S(1)}, u32[]{:S(2)}, u32[]{:S(2)}) collective-permute-start(bf16[1024,256]{1,0:T(8,128)(2,1)S(1)} %collective-permute-done.1.refs_7_), channel_id=1, source_target_pairs={{0,1},{1,0},{2,3},{3,2},{4,5},{5,4},{6,7},{7,6},{8,9},{9,8},{10,11... | collective-permute-start | bytes 1572872 | tf_op jit(solution)/shard_map/ppermute | solution.py:270
  27.7 10.7 %collective-permute-start.8 = (bf16[1024,256]{1,0:T(8,128)(2,1)S(1)}, bf16[1024,256]{1,0:T(8,128)(2,1)S(1)}, u32[]{:S(2)}, u32[]{:S(2)}) collective-permute-start(bf16[1024,256]{1,0:T(8,128)(2,1)S(1)} %collective-permute-done.7.refs_8_), channel_id=1, source_target_pairs={{0,4},{1,3},{4,8},{5,1},{8,12},{9,5},{12,14},{13,9},{14,10},{15,13... | collective-permute-start | bytes 1572872 | tf_op jit(solution)/shard_map/ppermute | solution.py:267
  32.8 11.2 %collective-permute-start.3 = (bf16[1024,256]{1,0:T(8,128)(2,1)S(1)}, bf16[1024,256]{1,0:T(8,128)(2,1)S(1)}, u32[]{:S(2)}, u32[]{:S(2)}) collective-permute-start(bf16[1024,256]{1,0:T(8,128)(2,1)S(1)} %collective-permute-done.2.refs_7_), channel_id=1, source_target_pairs={{0,4},{1,3},{4,8},{5,1},{8,12},{9,5},{12,14},{13,9},{14,10},{15,13... | collective-permute-start | bytes 1572872 | tf_op jit(solution)/shard_map/ppermute | solution.py:267
  40.1 3.9 %collective-permute-start.13 = (bf16[1024,256]{1,0:T(8,128)(2,1)S(1)}, bf16[1024,256]{1,0:T(8,128)(2,1)S(1)}, u32[]{:S(2)}, u32[]{:S(2)}) collective-permute-start(bf16[1024,256]{1,0:T(8,128)(2,1)S(1)} %collective-permute-done.8.refs_8_), channel_id=1, source_target_pairs={{0,1},{1,0},{2,3},{3,2},{4,5},{5,4},{6,7},{7,6},{8,9},{9,8},{10,11... | collective-permute-start | bytes 1572872 | tf_op jit(solution)/shard_map/ppermute | solution.py:270
  40.2 3.8 %collective-permute-start.14 = (bf16[1024,256]{1,0:T(8,128)(2,1)S(1)}, bf16[1024,256]{1,0:T(8,128)(2,1)S(1)}, u32[]{:S(2)}, u32[]{:S(2)}) collective-permute-start(bf16[1024,256]{1,0:T(8,128)(2,1)S(1)} %collective-permute-done.2.refs_7_), channel_id=1, source_target_pairs={{0,1},{1,0},{2,3},{3,2},{4,5},{5,4},{6,7},{7,6},{8,9},{9,8},{10,11... | collective-permute-start | bytes 1572872 | tf_op jit(solution)/shard_map/ppermute | solution.py:270
  44.0 2.4 %collective-permute-start.4 = (bf16[1024,256]{1,0:T(8,128)(2,1)S(1)}, bf16[1024,256]{1,0:T(8,128)(2,1)S(1)}, u32[]{:S(2)}, u32[]{:S(2)}) collective-permute-start(bf16[1024,256]{1,0:T(8,128)(2,1)S(1)} %collective-permute-done.3.refs_7_), channel_id=1, source_target_pairs={{0,1},{1,0},{2,3},{3,2},{4,5},{5,4},{6,7},{7,6},{8,9},{9,8},{10,11... | collective-permute-start | bytes 1572872 | tf_op jit(solution)/shard_map/ppermute | solution.py:270
  50.7 1.9 %collective-permute-start.15 = (bf16[48,4096]{1,0:T(8,128)(2,1)S(1)}, bf16[48,4096]{1,0:T(8,128)(2,1)S(1)}, u32[]{:S(2)}, u32[]{:S(2)}) collective-permute-start(bf16[48,4096]{1,0:T(8,128)(2,1)S(1)} %get-tuple-element.88), channel_id=1, source_target_pairs={{0,1},{1,0},{2,3},{3,2},{4,5},{5,4},{6,7},{7,6},{8,9},{9,8},{10,11... | collective-permute-start | bytes 1179656 | tf_op jit(solution)/shard_map/ppermute | solution.py:270
